TPU v7x, 128 devices: a whole 4x4x4 slice. The times are simulated.
128 devices in a mesh: dp: 16 (over z, x_hi, core), tensor: 8 (over x_lo, y).
Axes of the slice: x: 4 (x_hi: 2, x_lo: 2; x = x_hi * 2 + x_lo), y: 4, z: 4, core: 2. Of those that a mesh axis runs over, the one named last changes fastest.
Arguments:
- inputs: bfloat16 [12288, 2304], P('dp'), may hold values from -6 to 6
- up_pre: bfloat16 [12288, 18432], P('dp', 'tensor'), may hold values from -6 to 6
- gate_act: bfloat16 [12288, 18432], P('dp', 'tensor'), may hold values from -0.75 to 3.6
- out_grad: bfloat16 [12288, 2304], P('dp'), may hold values from -7.6546554 to 7.6546554
- down_weight: bfloat16 [2304, 18432], P('dp', 'tensor'), may hold values from -0.046875 to 0.046875
- noise_up: float32 [2304, 18432], P('dp', 'tensor'), may hold values from -48 to 48
- noise_down: float32 [2304, 18432], P('dp', 'tensor'), may hold values from -48 to 48
Outputs:
- up_update: float32 [2304, 18432], P('dp', 'tensor')
- down_update: float32 [2304, 18432], P('dp', 'tensor')
All inputs are finite; a program needn't handle non-finite values.
Results may differ from a plain program's by a relative error of at most 0.015.
Values may be sent and summed in bfloat16 or wider, within the bound.
No kernel may reach another device: no remote copies, remote signals or barrier semaphores. Data moves between devices by JAX's collectives and lax.ppermute only.
A program may use at most 256 MiB of HBM per device.

v0:
```python
import math

import jax
import jax.numpy as jnp
from jax import lax
from jax.sharding import PartitionSpec as P

D = 2304
FF = 18432
SEQ = 384


def clip_scale(partial_value):
    totals = lax.psum(partial_value, "tensor")
    clip_bound = 4.0 * math.sqrt(D * FF)
    return clip_bound / jnp.maximum(jnp.sqrt(totals), clip_bound)


def on_device(inputs, up_pre, gate_act, out_grad, down_weight, noise_up, noise_down):
    tok_rows, width = inputs.shape
    local_ff = up_pre.shape[1]
    examples = tok_rows // SEQ
    hidden = (gate_act.astype(jnp.float32) * up_pre.astype(jnp.float32)).astype(jnp.bfloat16)
    hidden_grad = jnp.dot(
        out_grad,
        lax.all_gather(down_weight, "dp", axis=0, tiled=True),
        preferred_element_type=jnp.float32,
    )
    act_grad = (hidden_grad * gate_act.astype(jnp.float32)).astype(jnp.bfloat16)
    x_ex = inputs.reshape(examples, SEQ, width)
    dy_ex = out_grad.reshape(examples, SEQ, width)
    hidden_ex = hidden.reshape(examples, SEQ, local_ff)
    act_ex = act_grad.reshape(examples, SEQ, local_ff)
    per_down = jnp.einsum("esr,esf->erf", dy_ex, hidden_ex, preferred_element_type=jnp.float32)
    per_up = jnp.einsum("esr,esf->erf", x_ex, act_ex, preferred_element_type=jnp.float32)
    partial_value = jnp.sum(per_down * per_down, axis=(1, 2)) + jnp.sum(
        per_up * per_up, axis=(1, 2)
    )
    scale = clip_scale(partial_value)
    rows = per_up
    up_sum = lax.psum_scatter(
        jnp.sum(scale[:, None, None] * rows, axis=0).astype(jnp.bfloat16),
        "dp",
        scatter_dimension=0,
        tiled=True,
    ).astype(jnp.float32)
    rows = per_down
    down_sum = lax.psum_scatter(
        jnp.sum(scale[:, None, None] * rows, axis=0).astype(jnp.bfloat16),
        "dp",
        scatter_dimension=0,
        tiled=True,
    ).astype(jnp.float32)
    total_examples = examples * lax.axis_size("dp")
    up_update = (up_sum + noise_up) / total_examples
    down_update = (down_sum + noise_down) / total_examples
    return (up_update, down_update)


def solution(mesh):
    in_specs = (
        P("dp", None),
        P("dp", "tensor"),
        P("dp", "tensor"),
        P("dp", None),
        P("dp", "tensor"),
        P("dp", "tensor"),
        P("dp", "tensor"),
    )
    out_specs = (P("dp", "tensor"), P("dp", "tensor"))
    return jax.shard_map(
        on_device, mesh=mesh, in_specs=in_specs, out_specs=out_specs, check_vma=False
    )
```

profile of v0, /device:TPU:1, one launch (start us, length us, event | category | flops | bytes accessed | tf_op | source)
XLA Modules:
  0.0 447.0 jit_solution(1150799245914900369)
XLA Ops:
  7.2 0.0 all-gather.2.cloned.1.call-start
  7.2 0.7 all-gather.2.cloned.1.call-update
  7.9 0.0 reduce-scatter.9.cloned.1.call-start
  8.0 5.9 %fusion = bf16[768,2304]{1,0:T(8,128)(2,1)} fusion(bf16[768,2304]{1,0:T(8,128)(2,1)} %param.9, bf16[768,2304]{1,0:T(8,128)(2,1)} %param.8), kind=kLoop, calls=%fused_computation.8 | loop fusion | flops 7077888 | bytes 10616832 | tf_op jit(solution)/shard_map/convert_element_type | solution.py:23
  13.9 20.1 %multiply_reduce_fusion.3 = (f32[2]{0:T(128)S(1)}, f32[2,2304,2304]{2,1,0:T(8,128)}) fusion(bf16[2,384,2304]{2,1,0:T(8,128)(2,1)} %bitcast.21, bf16[2,384,2304]{2,1,0:T(8,128)(2,1)S(1)} %bitcast.18), kind=kOutput, calls=%fused_computation.3 | convolution fusion | flops 8174960640 | bytes 49545224 | tf_op jit(solution)/shard_map/esr,esf->erf/dot_general | solution.py:34
  34.0 62.7 %all-gather.2.cloned.1.call-done = bf16[2304,2304]{1,0:T(8,128)(2,1)} async-done(((bf16[144,2304]{1,0:T(8,128)(2,1)}), bf16[2304,2304]{1,0:T(8,128)(2,1)}) %all-gather.2.cloned.1.call-update) | async-done | bytes 10616848 | tf_op jit(solution)/shard_map/all_gather | solution.py:26
  96.7 14.2 %fusion.1 = bf16[768,2304]{1,0:T(8,128)(2,1)} fusion(bf16[768,2304]{1,0:T(8,128)(2,1)} %param.9, bf16[768,2304]{1,0:T(8,128)(2,1)S(1)} %copy-done, bf16[2304,2304]{1,0:T(8,128)(2,1)} %all-gather.2.cloned.1.call-done), kind=kOutput, calls=%fused_computation.9 | convolution fusion | flops 8159035392 | bytes 21233664 | tf_op jit(solution)/shard_map/dot_general | solution.py:24
  110.9 23.8 %multiply_reduce_fusion.2 = (f32[2]{0:T(128)S(1)}, f32[2,2304,2304]{2,1,0:T(8,128)}) fusion(bf16[2,384,2304]{2,1,0:T(8,128)(2,1)} %bitcast.22, bf16[2,384,2304]{2,1,0:T(8,128)(2,1)} %bitcast.23), kind=kOutput, calls=%fused_computation.2 | convolution fusion | flops 8174960640 | bytes 49545224 | tf_op jit(solution)/shard_map/esr,esf->erf/dot_general | solution.py:35
  134.7 14.9 %psum.7 = f32[2]{0:T(128)S(1)} all-reduce(f32[2]{0:T(128)S(1)} %add.15), channel_id=1, replica_groups=mesh['dp'=16,'tensor'=8] {'tensor'}, use_global_device_ids=true, to_apply=%region_2.0 | all-reduce | flops 2 | bytes 16 | tf_op jit(solution)/shard_map/psum | solution.py:14
  149.6 38.6 %multiply_reduce_fusion = (bf16[2304,2304]{1,0:T(8,128)(2,1)}, bf16[2304,2304]{1,0:T(8,128)(2,1)}) fusion(f32[2,2304,2304]{2,1,0:T(8,128)} %get-tuple-element.9, f32[2]{0:T(128)S(1)} %maximum_divide_fusion, f32[2,2304,2304]{2,1,0:T(8,128)} %get-tuple-element.11), kind=kLoop, calls=%fused_computation | loop fusion | flops 31850496 | bytes 106168328 | tf_op jit(solution)/shard_map/reduce_sum | solution.py:49
  188.2 15.3 %copy.27 = bf16[2304,2304]{1,0:T(8,128)(2,1)} copy(bf16[2304,2304]{0,1:T(8,128)(2,1)} %bitcast.20) | data formatting | bytes 21233664
  203.5 0.0 reduce-scatter.7.cloned.1.call-start
  203.6 15.2 %copy.25 = bf16[2304,2304]{1,0:T(8,128)(2,1)} copy(bf16[2304,2304]{0,1:T(8,128)(2,1)} %bitcast.19) | data formatting | bytes 21233664
  218.7 0.0 reduce-scatter.7.cloned.1.call-update
  218.8 1.9 copy.20
  220.7 3.0 copy.19
  223.7 91.9 %reduce-scatter.9.cloned.1.call-done = bf16[144,2304]{1,0:T(8,128)(2,1)} async-done(((bf16[2304,2304]{1,0:T(8,128)(2,1)}), bf16[144,2304]{1,0:T(8,128)(2,1)}) %reduce-scatter.9.cloned.1.call-update) | async-done | bytes 663568
  315.5 1.5 copy.28
  317.0 1.7 add_multiply_fusion
  318.7 2.8 copy.22
  321.5 110.1 %reduce-scatter.7.cloned.1.call-done = bf16[144,2304]{1,0:T(8,128)(2,1)} async-done(((bf16[2304,2304]{1,0:T(8,128)(2,1)}), bf16[144,2304]{1,0:T(8,128)(2,1)}) %reduce-scatter.7.cloned.1.call-update) | async-done | bytes 663568
  431.6 2.4 copy.26
  434.0 3.7 add_multiply_fusion.1
  437.7 2.8 copy.21
  (7 shorter events, 0.0 us)
Async XLA Ops:
  7.2 6.7 %copy-start = (bf16[768,2304]{1,0:T(8,128)(2,1)S(1)}, bf16[768,2304]{1,0:T(8,128)(2,1)}, u32[]{:S(2)}) copy-start(bf16[768,2304]{1,0:T(8,128)(2,1)} %param.10) | copy-start | bytes 10616836
  7.2 89.5 %all-gather.2.cloned.1.call-start = ((), (), s32[]{:S(2)}) async-start(), calls=%async_computation.2 | async-start | bytes 11280384 | tf_op jit(solution)/shard_map/all_gather | solution.py:26
  7.9 307.6 %reduce-scatter.9.cloned.1.call-start = ((), (), s32[]{:S(2)}) async-start(), calls=%async_computation.4 | async-start | bytes 11280384
  203.5 228.0 %reduce-scatter.7.cloned.1.call-start = ((), (), s32[]{:S(2)}) async-start(), calls=%async_computation.3 | async-start | bytes 11280384
  431.6 8.9 %copy-start.1 = (bf16[768,2304]{1,0:T(8,128)(2,1)S(1)}, bf16[768,2304]{1,0:T(8,128)(2,1)}, u32[]{:S(2)}) copy-start(bf16[768,2304]{1,0:T(8,128)(2,1)} %param.10) | copy-start | bytes 10616836
Sparse Core Ops, SparseCore 0:
  10.5 86.1 all-gather.1
  203.7 111.8 reduce-scatter.8
  319.8 111.7 reduce-scatter.6
where the time goes:
time: 448 us; the launch traced here: 447 us
  waiting for transfers between devices  265 us (59%)
  matrix products  58 us (13%)
  other arithmetic  49.9 us (11%)
  local copies, waits for them, and re-layouts  44.9 us (10%)
  blocking collectives  14.9 us (3%)
  between operations  13.8 us (3%)
    unnamed x5, waiting for transfers between devices  203 us
    all_gather x1, waiting for transfers between devices, on_device(): lax.all_gather(down_weight, 'dp', axis=0, tiled=True)  62.7 us
    unnamed x12, local copies, waits for them, and re-layouts  44.9 us
    reduce_sum x1, other arithmetic, on_device(): jnp.sum(scale[:, None, None] * rows, axis=0).astype(jnp.bfloat16)  38.6 us
    dot_general x1, matrix products, on_device(): jnp.einsum('esr,esf->erf', x_ex, act_ex, preferred_element_type=jnp.float32)  23.8 us
    dot_general x1, matrix products, on_device(): jnp.einsum('esr,esf->erf', dy_ex, hidden_ex, preferred_element_type=jnp.f...  20.1 us
    psum x1, blocking collectives, clip_scale(): totals = lax.psum(partial_value, 'tensor')  14.9 us
    dot_general x1, matrix products, on_device(): jnp.dot(out_grad, lax.all_gather(down_weight, 'dp', axis=0, tiled=True),...  14.2 us
  transfers between devices with their start and end apart: 3, of which 3 were waited for; matrix products, arithmetic and copies ran while one was open for 12% of the time, Pallas kernels for 0%

commit v1 on v0

v1 whole, which is shorter than its diff:
```python
import math

import jax
import jax.numpy as jnp
from jax import lax
from jax.experimental import pallas as pl
from jax.experimental.pallas import tpu as pltpu
from jax.sharding import PartitionSpec as P

D = 2304
FF = 18432
SEQ = 384
N_DP = 16
N_TENSOR = 8
MIB = 1 << 20

Z_UP = [(i, (i + 4) % 16) for i in range(16)]
Z_DOWN = [(i, (i + 12) % 16) for i in range(16)]
X_SWAP = [(i, i ^ 2) for i in range(16)]
CORE_SWAP = [(i, i ^ 1) for i in range(16)]
Y_TURNS = [[(t, (t & 4) | ((t + k) & 3)) for t in range(8)] for k in (1, 2, 3)]
XLO_SWAP = [(t, t ^ 4) for t in range(8)]


def nt(a, b):
    return lax.dot_general(a, b, (((1,), (1,)), ((), ())), preferred_element_type=jnp.float32)


def nn(a, b):
    return lax.dot_general(a, b, (((1,), (0,)), ((), ())), preferred_element_type=jnp.float32)


def prep_kernel(half_ref, x_ref, dy_ref, gate_ref, up_ref, hid_ref, xt_ref, dyt_ref, gx_ref, vd_ref):
    del half_ref
    hid = (gate_ref[...].astype(jnp.float32) * up_ref[...].astype(jnp.float32)).astype(jnp.bfloat16)
    hid_ref[...] = hid
    x, dy = x_ref[...], dy_ref[...]
    xt_ref[...] = x.T
    dyt_ref[...] = dy.T
    gx_ref[0] = nt(x, x)
    vd_ref[...] = jnp.sum(nt(dy, dy) * nt(hid, hid), axis=0, keepdims=True)[None]


def prep(half, x, dy, gate, up):
    width, ff = x.shape[1], 1152
    split = gate.shape[1] // ff

    def col(i, h):
        return (i, h[0] if split > 1 else 0)

    return pl.pallas_call(
        prep_kernel,
        grid_spec=pltpu.PrefetchScalarGridSpec(
            num_scalar_prefetch=1,
            grid=(2,),
            in_specs=[
                pl.BlockSpec((SEQ, width), lambda i, h: (i, 0)),
                pl.BlockSpec((SEQ, width), lambda i, h: (i, 0)),
                pl.BlockSpec((SEQ, ff), col),
                pl.BlockSpec((SEQ, ff), col),
            ],
            out_specs=[
                pl.BlockSpec((SEQ, ff), lambda i, h: (i, 0)),
                pl.BlockSpec((width, SEQ), lambda i, h: (0, i)),
                pl.BlockSpec((width, SEQ), lambda i, h: (0, i)),
                pl.BlockSpec((1, SEQ, SEQ), lambda i, h: (i, 0, 0)),
                pl.BlockSpec((1, 1, SEQ), lambda i, h: (i, 0, 0)),
            ],
        ),
        out_shape=[
            jax.ShapeDtypeStruct((2 * SEQ, ff), jnp.bfloat16),
            jax.ShapeDtypeStruct((width, 2 * SEQ), jnp.bfloat16),
            jax.ShapeDtypeStruct((width, 2 * SEQ), jnp.bfloat16),
            jax.ShapeDtypeStruct((2, SEQ, SEQ), jnp.float32),
            jax.ShapeDtypeStruct((2, 1, SEQ), jnp.float32),
        ],
        compiler_params=pltpu.CompilerParams(vmem_limit_bytes=40 * MIB),
        cost_estimate=pl.CostEstimate(flops=7_000_000_000, bytes_accessed=20_000_000, transcendentals=0),
        name="prep",
    )(half, x, dy, gate, up)


N_PIECES = 9


def act_kernel(rows_ref, dya_ref, dyb_ref, ga_ref, gb_ref, gxa_ref, gxb_ref, *rest):
    pieces = rest[:N_PIECES]
    act_ref, vu_ref, w_ref, sems = rest[N_PIECES:]
    i = pl.program_id(0)

    @pl.when(i == 0)
    def _():
        copies = []
        for j, piece in enumerate(pieces):
            n = piece.shape[0]
            at = pl.multiple_of(rows_ref[j], 16)
            copies.append(pltpu.make_async_copy(piece, w_ref.at[pl.ds(at, n), :], sems.at[j]))
        for copy in copies:
            copy.start()
        for copy in copies:
            copy.wait()

    def example(dy_ref, gate_ref, gx_ref):
        grad = nn(dy_ref[...], w_ref[...])
        act = (grad * gate_ref[...].astype(jnp.float32)).astype(jnp.bfloat16)
        act_ref[...] = act
        vu_ref[...] = jnp.sum(gx_ref[0] * nt(act, act), axis=0, keepdims=True)[None]

    @pl.when(i < 2)
    def _():
        example(dya_ref, ga_ref, gxa_ref)

    @pl.when(i >= 2)
    def _():
        example(dyb_ref, gb_ref, gxb_ref)


def act_grads(scalars, dy_a, dy_b, gate_a, gate_b, gx_a, gx_b, pieces):
    width, ff = dy_a.shape[1], 1152

    def first(i, s):
        return jnp.minimum(i, 1)

    def second(i, s):
        return jnp.maximum(i - 2, 0)

    return pl.pallas_call(
        act_kernel,
        grid_spec=pltpu.PrefetchScalarGridSpec(
            num_scalar_prefetch=1,
            grid=(4,),
            in_specs=[
                pl.BlockSpec((SEQ, width), lambda i, s: (first(i, s), 0)),
                pl.BlockSpec((SEQ, width), lambda i, s: (second(i, s), 0)),
                pl.BlockSpec((SEQ, ff), lambda i, s: (first(i, s), s[N_PIECES])),
                pl.BlockSpec((SEQ, ff), lambda i, s: (second(i, s), 0)),
                pl.BlockSpec((1, SEQ, SEQ), lambda i, s: (first(i, s), 0, 0)),
                pl.BlockSpec((1, SEQ, SEQ), lambda i, s: (second(i, s), 0, 0)),
            ]
            + [pl.BlockSpec(memory_space=pl.ANY)] * N_PIECES,
            out_specs=[
                pl.BlockSpec((SEQ, ff), lambda i, s: (i, 0)),
                pl.BlockSpec((1, 1, SEQ), lambda i, s: (i, 0, 0)),
            ],
            scratch_shapes=[pltpu.VMEM((width, ff), jnp.bfloat16), pltpu.SemaphoreType.DMA((N_PIECES,))],
        ),
        out_shape=[
            jax.ShapeDtypeStruct((4 * SEQ, ff), jnp.bfloat16),
            jax.ShapeDtypeStruct((4, 1, SEQ), jnp.float32),
        ],
        compiler_params=pltpu.CompilerParams(vmem_limit_bytes=40 * MIB),
        cost_estimate=pl.CostEstimate(flops=10_000_000_000, bytes_accessed=25_000_000, transcendentals=0),
        name="act_grads",
    )(scalars, dy_a, dy_b, gate_a, gate_b, gx_a, gx_b, *pieces)


def share_kernel(chunk_ref, clip_ref, la_ref, lb_ref, ra_ref, rb_ref, out_ref, sa_ref, sb_ref):
    del chunk_ref

    @pl.when(pl.program_id(0) == 0)
    def _():
        for e in range(2):
            rows = pl.ds(e * SEQ, SEQ)
            sa_ref[rows, :] = (ra_ref[rows, :].astype(jnp.float32) * clip_ref[e]).astype(jnp.bfloat16)
            sb_ref[rows, :] = (rb_ref[rows, :].astype(jnp.float32) * clip_ref[2 + e]).astype(jnp.bfloat16)

    out_ref[0] = (nn(la_ref[...], sa_ref[...]) + nn(lb_ref[...], sb_ref[...])).astype(out_ref.dtype)


def shares(chunks, clip, lhs_a, lhs_b, rhs_a, rhs_b, b_block, rows, dtype, name):
    n, ff, tok = chunks.shape[0], rhs_a.shape[1], 2 * SEQ
    return pl.pallas_call(
        share_kernel,
        grid_spec=pltpu.PrefetchScalarGridSpec(
            num_scalar_prefetch=2,
            grid=(n,),
            in_specs=[
                pl.BlockSpec((rows, tok), lambda i, s, c: (s[i], 0)),
                pl.BlockSpec((rows, tok), lambda i, s, c: (s[i], 0)),
                pl.BlockSpec((tok, ff), lambda i, s, c: (0, 0)),
                pl.BlockSpec((tok, ff), lambda i, s, c: (b_block, 0)),
            ],
            out_specs=pl.BlockSpec((1, rows, ff), lambda i, s, c: (i, 0, 0)),
            scratch_shapes=[pltpu.VMEM((tok, ff), jnp.bfloat16)] * 2,
        ),
        out_shape=jax.ShapeDtypeStruct((n, rows, ff), dtype),
        compiler_params=pltpu.CompilerParams(vmem_limit_bytes=40 * MIB),
        cost_estimate=pl.CostEstimate(flops=n * 1_020_000_000, bytes_accessed=15_000_000, transcendentals=0),
        name=name,
    )(chunks, clip, lhs_a, lhs_b, rhs_a, rhs_b)


def on_device(inputs, up_pre, gate_act, out_grad, down_weight, noise_up, noise_down):
    f32, bf16 = jnp.float32, jnp.bfloat16
    width, local_ff = inputs.shape[1], up_pre.shape[1]
    ff = local_ff // 2
    own_rows = down_weight.shape[0]
    rows = 2 * own_rows
    me = lax.axis_index("dp")
    core, x, z = me % 2, (me // 2) % 2, me // 4

    def chip(dz, dx):
        return ((z + dz) % 4) * 2 + ((x + dx) % 2)

    def half_cols(a, which):
        return lax.dynamic_slice(a, (0, which * ff), (a.shape[0], ff))

    def go(a, perm):
        return lax.ppermute(a, "dp", perm)

    w_mine = half_cols(down_weight, core)
    w_other = go(half_cols(down_weight, 1 - core), CORE_SWAP)
    own = jnp.where(core == 0, jnp.concatenate([w_mine, w_other]), jnp.concatenate([w_other, w_mine]))
    w_zm = go(own, Z_UP)
    w_zp = go(own, Z_DOWN)
    w_x = go(own, X_SWAP)
    w_z2_top = go(w_zm[:own_rows], Z_UP)
    w_z2_bot = go(w_zp[own_rows:], Z_DOWN)
    w_zm_x = go(w_x, Z_UP)
    w_zp_x = go(w_x, Z_DOWN)
    w_z2_x = go(jnp.concatenate([w_z2_top, w_z2_bot]), X_SWAP)
    pieces = [own, w_zm, w_zp, w_x, w_z2_top, w_z2_bot, w_zm_x, w_zp_x, w_z2_x]
    places = [
        chip(0, 0) * rows,
        chip(3, 0) * rows,
        chip(1, 0) * rows,
        chip(0, 1) * rows,
        chip(2, 0) * rows,
        chip(2, 0) * rows + own_rows,
        chip(3, 1) * rows,
        chip(1, 1) * rows,
        chip(2, 1) * rows,
    ]

    dy_b = go(out_grad, CORE_SWAP)
    x_b = go(inputs, CORE_SWAP)
    gate_b = go(half_cols(gate_act, 1 - core), CORE_SWAP)
    up_b = go(half_cols(up_pre, 1 - core), CORE_SWAP)

    half = jnp.stack([core]).astype(jnp.int32)
    hid_a, xt_a, dyt_a, gx_a, vd_a = prep(half, inputs, out_grad, gate_act, up_pre)
    hid_b, xt_b, dyt_b, gx_b, vd_b = prep(half, x_b, dy_b, gate_b, up_b)

    scalars = jnp.stack(places + [core]).astype(jnp.int32)
    act, vu = act_grads(scalars, out_grad, dy_b, gate_act, gate_b, gx_a, gx_b, pieces)

    part = jnp.sum(jnp.concatenate([vd_a, vd_b]) + vu, axis=(1, 2))
    part = part + jnp.roll(lax.ppermute(part, "dp", CORE_SWAP), 2)
    part = part + lax.ppermute(part, "tensor", XLO_SWAP)
    turns = [lax.ppermute(part, "tensor", perm) for perm in Y_TURNS]
    sq_norm = jnp.maximum(part + (turns[0] + turns[2]) + turns[1], 0.0)
    clip_bound = 4.0 * math.sqrt(D * FF)
    clip = clip_bound / jnp.maximum(jnp.sqrt(sq_norm), clip_bound)

    early = jnp.stack([chip(2, 1), chip(1, 1), chip(3, 1)]).astype(jnp.int32)
    late = jnp.stack([chip(2, 0), chip(0, 1), chip(1, 0), chip(3, 0), chip(0, 0)]).astype(jnp.int32)

    def first_part(lhs_a, lhs_b, rhs_a, rhs_b, b_block, name):
        out = shares(early, clip, lhs_a, lhs_b, rhs_a, rhs_b, b_block, rows, bf16, name)
        return go(out[0], X_SWAP), go(out[1], Z_UP), go(out[2], Z_DOWN)

    def second_part(lhs_a, lhs_b, rhs_a, rhs_b, b_block, name):
        return shares(late, clip, lhs_a, lhs_b, rhs_a, rhs_b, b_block, rows, f32, name)

    def reduce_on(got, mine):
        r1, r2p, r2m = got
        s3 = (mine[0] + r1.astype(f32)).astype(bf16)
        r3p = go(s3[:own_rows], Z_UP)
        r3m = go(s3[own_rows:], Z_DOWN)
        s4 = (mine[1] + r2p.astype(f32) + r2m.astype(f32)).astype(bf16)
        r4 = go(s4, X_SWAP)
        s5p = jnp.concatenate([mine[2, :own_rows] + r3p.astype(f32), mine[2, own_rows:]]).astype(bf16)
        s5m = jnp.concatenate([mine[3, :own_rows], mine[3, own_rows:] + r3m.astype(f32)]).astype(bf16)
        r5p = go(s5p, Z_UP)
        r5m = go(s5m, Z_DOWN)
        return mine[4] + r4.astype(f32) + r5p.astype(f32) + r5m.astype(f32)

    down_args = (dyt_a, dyt_b, hid_a, hid_b, 0)
    up_args = (xt_a, xt_b, act, act, 1)
    got_down = first_part(*down_args, "down_first")
    got_up = first_part(*up_args, "up_first")
    mine_down = second_part(*down_args, "down_second")
    mine_up = second_part(*up_args, "up_second")
    sum_down = reduce_on(got_down, mine_down)
    sum_up = reduce_on(got_up, mine_up)

    def finish(total, noise):
        mine = lax.dynamic_slice(total, (core * own_rows, 0), (own_rows, ff))
        other = go(lax.dynamic_slice(total, ((1 - core) * own_rows, 0), (own_rows, ff)), CORE_SWAP)
        whole = jnp.where(
            core == 0, jnp.concatenate([mine, other], axis=1), jnp.concatenate([other, mine], axis=1)
        )
        return (whole + noise) / (2 * N_DP)

    down_update = finish(sum_down, noise_down)
    up_update = finish(sum_up, noise_up)
    return (up_update, down_update)


def solution(mesh):
    in_specs = (
        P("dp", None),
        P("dp", "tensor"),
        P("dp", "tensor"),
        P("dp", None),
        P("dp", "tensor"),
        P("dp", "tensor"),
        P("dp", "tensor"),
    )
    out_specs = (P("dp", "tensor"), P("dp", "tensor"))
    return jax.shard_map(
        on_device, mesh=mesh, in_specs=in_specs, out_specs=out_specs, check_vma=False
    )
```

time: 448 us -> 226 us (0.50)
  waiting for transfers between devices: 265 us -> 60 us
  Pallas kernels: 0 us -> 64 us
  starting transfers between devices: 0.12 us -> 60.5 us
  matrix products: 58 us -> 0 us
  other arithmetic: 49.9 us -> 12.4 us
  local copies, waits for them, and re-layouts: 44.9 us -> 27.6 us
  blocking collectives: 14.9 us -> 0 us
  between operations: 13.8 us -> 1.18 us
    unnamed x5 -> x0, waiting for transfers between devices: 203 us -> none
    pallas_call x0 -> x7, Pallas kernels: none -> 64 us  [the longest x4 27.8 us: shares(): pl.pallas_call(share_kernel, grid_spec=pltpu.PrefetchScalarGridSpec(num_s...]
    all_gather x1 -> x0, waiting for transfers between devices: 62.7 us -> none  [on_device(): lax.all_gather(down_weight, 'dp', axis=0, tiled=True)]
    ppermute x0 -> x36, starting transfers between devices: none -> 60.5 us  [the longest x31 51.5 us: go(): return lax.ppermute(a, 'dp', perm)]
    ppermute x0 -> x36, waiting for transfers between devices: none -> 60 us  [the longest x31 54.2 us: go(): return lax.ppermute(a, 'dp', perm)]
    dot_general x3 -> x0, matrix products: 58 us -> none  [the longest x1 23.8 us: on_device(): jnp.einsum('esr,esf->erf', x_ex, act_ex, preferred_element_type=jnp.float32)]
    reduce_sum x1, other arithmetic: 38.6 us -> 0.12 us  [on_device(): part = jnp.sum(jnp.concatenate([vd_a, vd_b]) + vu, axis=(1, 2))]
    unnamed x12 -> x62, local copies, waits for them, and re-layouts: 44.9 us -> 20.1 us
  transfers between devices with their start and end apart: 3 -> 36, of which waited for: 3 -> 18; matrix products, arithmetic and copies ran while one was open for 12% -> 8% of each run, Pallas kernels for 0% -> 17%
where the time goes in v1:
time: 226 us
  Pallas kernels  64 us (28%)
  starting transfers between devices  60.5 us (27%)
  waiting for transfers between devices  60 us (27%)
  local copies, waits for them, and re-layouts  27.6 us (12%)
  other arithmetic  12.4 us (5%)
    ppermute x31, waiting for transfers between devices, go(): return lax.ppermute(a, 'dp', perm)  54.2 us
    ppermute x31, starting transfers between devices, go(): return lax.ppermute(a, 'dp', perm)  51.5 us
    pallas_call x4, Pallas kernels, shares(): pl.pallas_call(share_kernel, grid_spec=pltpu.PrefetchScalarGridSpec(num_s...  27.8 us
    unnamed x62, local copies, waits for them, and re-layouts  20.1 us
    pallas_call x1, Pallas kernels, act_grads(): pl.pallas_call(act_kernel, grid_spec=pltpu.PrefetchScalarGridSpec(num_sca...  20 us
    pallas_call x2, Pallas kernels, prep(): pl.pallas_call(prep_kernel, grid_spec=pltpu.PrefetchScalarGridSpec(num_sc...  16.2 us
    another operation x4, other arithmetic  6.76 us
    dynamic_slice x3, local copies, waits for them, and re-layouts, half_cols(): return lax.dynamic_slice(a, (0, which * ff), (a.shape[0], ff))  5.32 us
  transfers between devices with their start and end apart: 36, of which 18 were waited for; matrix products, arithmetic and copies ran while one was open for 8% of the time, Pallas kernels for 17%

profile of v1, /device:TPU:1, one launch (start us, length us, event | category | flops | bytes accessed | tf_op | source)
XLA Modules:
  0.0 225.7 jit_solution(1506063185263989381)
XLA Ops:
  3.8 5.1 %collective-permute-done.4 = bf16[144,1152]{1,0:T(8,128)(2,1)S(1)} collective-permute-done((bf16[144,1152]{1,0:T(8,128)(2,1)S(1)}, bf16[144,1152]{1,0:T(8,128)(2,1)S(1)}, u32[]{:S(2)}, u32[]{:S(2)}) %collective-permute-start.4) | collective-permute-done | bytes 331808 | tf_op jit(solution)/shard_map/ppermute | solution.py:209
  9.1 2.9 %collective-permute-start.7 = (bf16[288,1152]{1,0:T(8,128)(2,1)S(1)}, bf16[288,1152]{1,0:T(8,128)(2,1)}, u32[]{:S(2)}, u32[]{:S(2)}) collective-permute-start(bf16[288,1152]{1,0:T(8,128)(2,1)S(1)} %maximum_select_fusion.2.rest_0_), channel_id=1, source_target_pairs={{0,16},{8,24},{16,0},{24,8},{32,48},{40,56},{48,32},{56,40},{64,80... | collective-permute-start | bytes 1990664 | tf_op jit(solution)/shard_map/ppermute | solution.py:209
  12.0 3.8 %collective-permute-start.6 = (bf16[288,1152]{1,0:T(8,128)(2,1)S(1)}, bf16[288,1152]{1,0:T(8,128)(2,1)S(1)}, u32[]{:S(2)}, u32[]{:S(2)}) collective-permute-start(bf16[288,1152]{1,0:T(8,128)(2,1)S(1)} %maximum_select_fusion.2.rest_0_), channel_id=1, source_target_pairs={{0,96},{8,104},{16,112},{24,120},{32,0},{40,8},{48,16},{56,24},{64... | collective-permute-start | bytes 1990664 | tf_op jit(solution)/shard_map/ppermute | solution.py:209
  15.8 2.8 %constant_dynamic-slice_fusion.6 = bf16[768,1152]{1,0:T(8,128)(2,1)} fusion(bf16[768,2304]{1,0:T(8,128)(2,1)} %up_ref.1, s32[]{:T(128)S(6)} %select_n.145), kind=kLoop, calls=%fused_computation.64 | loop fusion | bytes 3538948 | tf_op jit(solution)/shard_map/dynamic_slice | solution.py:206
  20.0 6.9 %collective-permute-done.7.rest_3_ = bf16[288,1152]{1,0:T(8,128)(2,1)} collective-permute-done((bf16[288,1152]{1,0:T(8,128)(2,1)S(1)}, bf16[288,1152]{1,0:T(8,128)(2,1)}, u32[]{:S(2)}, u32[]{:S(2)}) %collective-permute-start.7) | collective-permute-done | bytes 663584 | tf_op jit(solution)/shard_map/ppermute | solution.py:209
  30.9 4.4 %collective-permute-done.5.rest_1_ = bf16[288,1152]{1,0:T(8,128)(2,1)S(1)} collective-permute-done((bf16[288,1152]{1,0:T(8,128)(2,1)S(1)}, bf16[288,1152]{1,0:T(8,128)(2,1)S(1)}, u32[]{:S(2)}, u32[]{:S(2)}) %collective-permute-start.5) | collective-permute-done | bytes 663584 | tf_op jit(solution)/shard_map/ppermute | solution.py:209
  35.5 7.3 %collective-permute-done.9.rest_5_ = bf16[144,1152]{1,0:T(8,128)(2,1)S(1)} collective-permute-done((bf16[144,1152]{1,0:T(8,128)(2,1)S(1)}, bf16[144,1152]{1,0:T(8,128)(2,1)S(1)}, u32[]{:S(2)}, u32[]{:S(2)}) %collective-permute-start.9) | collective-permute-done | bytes 331808 | tf_op jit(solution)/shard_map/ppermute | solution.py:209
  45.5 7.8 %prep.2 = (bf16[768,1152]{1,0:T(8,128)(2,1)S(1)}, bf16[2304,768]{1,0:T(8,128)(2,1)S(1)}, bf16[2304,768]{1,0:T(8,128)(2,1)S(1)}, f32[2,384,384]{2,1,0:T(8,128)S(1)}, f32[2,1,384]{2,1,0:T(1,128)S(1)}) custom-call(s32[1]{0:T(128)} %bitcast.5.half_ref, bf16[768,2304]{1,0:T(8,128)(2,1)S(1)} %copy-done.19, bf16[768,2304]{1,0:T(8,128)(2,1)} %dya_ref.1, ...), custom_call_target="tpu_custom_call" | custom-call | flops 7000000000 | bytes 20000000 | tf_op jit(solution)/shard_map/prep/pallas_call | solution.py:51
  61.0 8.4 %prep.3 = (bf16[768,1152]{1,0:T(8,128)(2,1)S(1)}, bf16[2304,768]{1,0:T(8,128)(2,1)S(1)}, bf16[2304,768]{1,0:T(8,128)(2,1)S(1)}, f32[2,384,384]{2,1,0:T(8,128)S(1)}, f32[2,1,384]{2,1,0:T(1,128)S(1)}) custom-call(s32[1]{0:T(128)} %bitcast.5.half_ref, bf16[768,2304]{1,0:T(8,128)(2,1)} %collective-permute-done.x_ref, ...), custom_call_target="tpu_custom_call" | custom-call | flops 7000000000 | bytes 20000000 | tf_op jit(solution)/shard_map/prep/pallas_call | solution.py:51
  76.6 20.0 %act_grads.1 = (bf16[1536,1152]{1,0:T(8,128)(2,1)S(1)}, f32[4,1,384]{2,1,0:T(1,128)S(1)}) custom-call(s32[10]{0:T(128)S(1)} %stack.80.rows_ref, bf16[768,2304]{1,0:T(8,128)(2,1)} %dya_ref.1, bf16[768,2304]{1,0:T(8,128)(2,1)} %collective-permute-done.1.dy_ref.dyb_ref, bf16[768,2304]{1,0:T(8,128)(2,1)} %ga_ref.1, ...), custom_call_target="tpu_custom_call" | custom-call | flops 10000000000 | bytes 25000000 | tf_op jit(solution)/shard_map/act_grads/pallas_call | solution.py:127
  96.8 4.3 %collective-permute-start.13 = (f32[4]{0:T(128)S(1)}, f32[4]{0:T(128)S(1)}, u32[]{:S(2)}, u32[]{:S(2)}) collective-permute-start(f32[4]{0:T(128)S(1)} %fusion.28), channel_id=1, source_target_pairs={{0,8},{8,0},{16,24},{24,16},{32,40},{40,32},{48,56},{56,48},{64,72... | collective-permute-start | bytes 56 | tf_op jit(solution)/shard_map/ppermute | solution.py:248
  104.5 2.9 %collective-permute-start.17 = (f32[4]{0:T(128)S(1)}, f32[4]{0:T(128)S(1)}, u32[]{:S(2)}, u32[]{:S(2)}) collective-permute-start(f32[4]{0:T(128)S(1)} %add.233), channel_id=1, source_target_pairs={{0,2},{1,3},{2,0},{3,1},{4,6},{5,7},{6,4},{7,5},{8,10},{9,11},{10,... | collective-permute-start | bytes 56 | tf_op jit(solution)/shard_map/ppermute | solution.py:250
  118.7 5.1 %down_first.1 = bf16[3,288,1152]{2,1,0:T(8,128)(2,1)S(1)} custom-call(s32[3]{0:T(128)S(1)} %pad_add_fusion.chunk_ref, f32[4]{0:T(128)S(1)} %maximum_divide_fusion.clip_ref, bf16[2304,768]{1,0:T(8,128)(2,1)S(1)} %copy-done.1, bf16[2304,768]{1,0:T(8,128)(2,1)S(1)} %copy-done.3, bf16[768,1152]{1,0:T(8,128)(2,1)S(1)} %copy-done.5, bf16[768,1152]{1,0:T(8,128)(2,1)S(1)} %copy-done.7), custom_call_target="tpu_custom_call" | custom-call | flops 3060000000 | bytes 15000000 | tf_op jit(solution)/shard_map/down_first/pallas_call | solution.py:172
  125.8 5.1 %up_first.1 = bf16[3,288,1152]{2,1,0:T(8,128)(2,1)S(1)} custom-call(s32[3]{0:T(128)S(1)} %pad_add_fusion.chunk_ref, f32[4]{0:T(128)S(1)} %maximum_divide_fusion.clip_ref, bf16[2304,768]{1,0:T(8,128)(2,1)S(1)} %get-tuple-element.19.la_ref, bf16[2304,768]{1,0:T(8,128)(2,1)S(1)} %get-tuple-element.20.lb_ref, ...), custom_call_target="tpu_custom_call" | custom-call | flops 3060000000 | bytes 15000000 | tf_op jit(solution)/shard_map/up_first/pallas_call | solution.py:172
  130.9 8.8 %up_second.1 = f32[5,288,1152]{2,1,0:T(8,128)} custom-call(s32[5]{0:T(128)S(1)} %stack.69.chunk_ref, f32[4]{0:T(128)S(1)} %maximum_divide_fusion.clip_ref, bf16[2304,768]{1,0:T(8,128)(2,1)S(1)} %get-tuple-element.19.la_ref, bf16[2304,768]{1,0:T(8,128)(2,1)S(1)} %get-tuple-element.20.lb_ref, bf16[1536,1152]{1,0:T(8,128)(2,1)S(1)} %get-tuple-element.21.ra_ref.rb_ref, ...), custom_call_target="tpu_custom_call" | custom-call | flops 5100000256 | bytes 15000000 | tf_op jit(solution)/shard_map/up_second/pallas_call | solution.py:172
  145.1 3.2 %convert.29 = bf16[5,288,1152]{2,1,0:T(8,128)(2,1)S(1)} convert(f32[5,288,1152]{2,1,0:T(8,128)} %up_second.1) | non-fusion elementwise | flops 1658880 | bytes 9953280 | tf_op jit(solution)/shard_map/convert.15
  148.4 8.8 %down_second.1 = f32[5,288,1152]{2,1,0:T(8,128)} custom-call(s32[5]{0:T(128)S(1)} %stack.69.chunk_ref, f32[4]{0:T(128)S(1)} %maximum_divide_fusion.clip_ref, bf16[2304,768]{1,0:T(8,128)(2,1)S(1)} %copy-done.1, bf16[2304,768]{1,0:T(8,128)(2,1)S(1)} %copy-done.3, bf16[768,1152]{1,0:T(8,128)(2,1)S(1)} %copy-done.5, bf16[768,1152]{1,0:T(8,128)(2,1)S(1)} %copy-done.7), custom_call_target="tpu_custom_call" | custom-call | flops 5100000256 | bytes 15000000 | tf_op jit(solution)/shard_map/down_second/pallas_call | solution.py:172
  157.2 3.2 %convert.32 = bf16[5,288,1152]{2,1,0:T(8,128)(2,1)S(1)} convert(f32[5,288,1152]{2,1,0:T(8,128)} %down_second.1) | non-fusion elementwise | flops 1658880 | bytes 9953280 | tf_op jit(solution)/shard_map/convert.7
  166.2 7.5 %collective-permute-done.28 = bf16[288,1152]{1,0:T(8,128)(2,1)S(1)} collective-permute-done((bf16[288,1152]{1,0:T(8,128)(2,1)S(1)}, bf16[288,1152]{1,0:T(8,128)(2,1)S(1)}, u32[]{:S(2)}, u32[]{:S(2)}) %collective-permute-start.28) | collective-permute-done | bytes 663584 | tf_op jit(solution)/shard_map/ppermute | solution.py:209
  183.5 4.4 %collective-permute-done.33 = bf16[144,1152]{1,0:T(8,128)(2,1)S(1)} collective-permute-done((bf16[144,1152]{1,0:T(8,128)(2,1)S(1)}, bf16[144,1152]{1,0:T(8,128)(2,1)S(1)}, u32[]{:S(2)}, u32[]{:S(2)}) %collective-permute-start.33) | collective-permute-done | bytes 331808 | tf_op jit(solution)/shard_map/ppermute | solution.py:209
  190.5 7.9 %collective-permute-done.20 = bf16[288,1152]{1,0:T(8,128)(2,1)S(1)} collective-permute-done((bf16[288,1152]{1,0:T(8,128)(2,1)S(1)}, bf16[288,1152]{1,0:T(8,128)(2,1)S(1)}, u32[]{:S(2)}, u32[]{:S(2)}) %collective-permute-start.20) | collective-permute-done | bytes 663584 | tf_op jit(solution)/shard_map/ppermute | solution.py:209
  198.4 3.7 %collective-permute-done.25 = bf16[288,1152]{1,0:T(8,128)(2,1)S(1)} collective-permute-done((bf16[288,1152]{1,0:T(8,128)(2,1)S(1)}, bf16[288,1152]{1,0:T(8,128)(2,1)S(1)}, u32[]{:S(2)}, u32[]{:S(2)}) %collective-permute-start.25) | collective-permute-done | bytes 663584 | tf_op jit(solution)/shard_map/ppermute | solution.py:209
  202.5 11.1 %collective-permute-start.26 = (f32[144,1152]{1,0:T(8,128)S(1)}, f32[144,1152]{1,0:T(8,128)S(1)}, u32[]{:S(2)}, u32[]{:S(2)}) collective-permute-start(f32[144,1152]{1,0:T(8,128)S(1)} %get-tuple-element.47), channel_id=1, source_target_pairs={{0,8},{8,0},{16,24},{24,16},{32,40},{40,32},{48,56},{56,48},{64,72... | collective-permute-start | bytes 1990664 | tf_op jit(solution)/shard_map/ppermute | solution.py:209
  216.7 6.0 %collective-permute-start.35 = (f32[144,1152]{1,0:T(8,128)S(1)}, f32[144,1152]{1,0:T(8,128)S(1)}, u32[]{:S(2)}, u32[]{:S(2)}) collective-permute-start(f32[144,1152]{1,0:T(8,128)S(1)} %get-tuple-element.45), channel_id=1, source_target_pairs={{0,8},{8,0},{16,24},{24,16},{32,40},{40,32},{48,56},{56,48},{64,72... | collective-permute-start | bytes 1990664 | tf_op jit(solution)/shard_map/ppermute | solution.py:209
  (155 shorter events, 73.2 us)
Async XLA Ops:
  0.6 60.3 %collective-permute-start = (bf16[768,2304]{1,0:T(8,128)(2,1)}, bf16[768,2304]{1,0:T(8,128)(2,1)}, u32[]{:S(2)}, u32[]{:S(2)}) collective-permute-start(bf16[768,2304]{1,0:T(8,128)(2,1)} %x_ref.1), channel_id=1, source_target_pairs={{0,8},{8,0},{16,24},{24,16},{32,40},{40,32},{48,56},{56,48},{64,72... | collective-permute-start | bytes 10616840 | tf_op jit(solution)/shard_map/ppermute | solution.py:209
  2.1 58.8 %collective-permute-start.1 = (bf16[768,2304]{1,0:T(8,128)(2,1)}, bf16[768,2304]{1,0:T(8,128)(2,1)}, u32[]{:S(2)}, u32[]{:S(2)}) collective-permute-start(bf16[768,2304]{1,0:T(8,128)(2,1)} %dya_ref.1), channel_id=1, source_target_pairs={{0,8},{8,0},{16,24},{24,16},{32,40},{40,32},{48,56},{56,48},{64,72... | collective-permute-start | bytes 10616840 | tf_op jit(solution)/shard_map/ppermute | solution.py:209
  9.1 17.8 %collective-permute-start.7 = (bf16[288,1152]{1,0:T(8,128)(2,1)S(1)}, bf16[288,1152]{1,0:T(8,128)(2,1)}, u32[]{:S(2)}, u32[]{:S(2)}) collective-permute-start(bf16[288,1152]{1,0:T(8,128)(2,1)S(1)} %maximum_select_fusion.2.rest_0_), channel_id=1, source_target_pairs={{0,16},{8,24},{16,0},{24,8},{32,48},{40,56},{48,32},{56,40},{64,80... | collective-permute-start | bytes 1990664 | tf_op jit(solution)/shard_map/ppermute | solution.py:209
  12.0 17.4 %collective-permute-start.6 = (bf16[288,1152]{1,0:T(8,128)(2,1)S(1)}, bf16[288,1152]{1,0:T(8,128)(2,1)S(1)}, u32[]{:S(2)}, u32[]{:S(2)}) collective-permute-start(bf16[288,1152]{1,0:T(8,128)(2,1)S(1)} %maximum_select_fusion.2.rest_0_), channel_id=1, source_target_pairs={{0,96},{8,104},{16,112},{24,120},{32,0},{40,8},{48,16},{56,24},{64... | collective-permute-start | bytes 1990664 | tf_op jit(solution)/shard_map/ppermute | solution.py:209
  18.6 16.7 %collective-permute-start.5 = (bf16[288,1152]{1,0:T(8,128)(2,1)S(1)}, bf16[288,1152]{1,0:T(8,128)(2,1)S(1)}, u32[]{:S(2)}, u32[]{:S(2)}) collective-permute-start(bf16[288,1152]{1,0:T(8,128)(2,1)S(1)} %maximum_select_fusion.2.rest_0_), channel_id=1, source_target_pairs={{0,32},{8,40},{16,48},{24,56},{32,64},{40,72},{48,80},{56,88},{64,... | collective-permute-start | bytes 1990664 | tf_op jit(solution)/shard_map/ppermute | solution.py:209
  26.9 33.2 %collective-permute-start.2 = (bf16[768,1152]{1,0:T(8,128)(2,1)}, bf16[768,1152]{1,0:T(8,128)(2,1)}, u32[]{:S(2)}, u32[]{:S(2)}) collective-permute-start(bf16[768,1152]{1,0:T(8,128)(2,1)} %constant_dynamic-slice_fusion.7), channel_id=1, source_target_pairs={{0,8},{8,0},{16,24},{24,16},{32,40},{40,32},{48,56},{56,48},{64,72... | collective-permute-start | bytes 5308424 | tf_op jit(solution)/shard_map/ppermute | solution.py:209
  29.4 30.8 %collective-permute-start.3 = (bf16[768,1152]{1,0:T(8,128)(2,1)}, bf16[768,1152]{1,0:T(8,128)(2,1)}, u32[]{:S(2)}, u32[]{:S(2)}) collective-permute-start(bf16[768,1152]{1,0:T(8,128)(2,1)} %constant_dynamic-slice_fusion.6), channel_id=1, source_target_pairs={{0,8},{8,0},{16,24},{24,16},{32,40},{40,32},{48,56},{56,48},{64,72... | collective-permute-start | bytes 5308424 | tf_op jit(solution)/shard_map/ppermute | solution.py:209
  42.8 14.5 %collective-permute-start.8 = (bf16[144,1152]{1,0:T(8,128)(2,1)S(1)}, bf16[144,1152]{1,0:T(8,128)(2,1)S(1)}, u32[]{:S(2)}, u32[]{:S(2)}) collective-permute-start(bf16[144,1152]{1,0:T(8,128)(2,1)S(1)} %slice.118), channel_id=1, source_target_pairs={{0,32},{8,40},{16,48},{24,56},{32,64},{40,72},{48,80},{56,88},{64,... | collective-permute-start | bytes 995336 | tf_op jit(solution)/shard_map/ppermute | solution.py:209
  57.3 16.1 %collective-permute-start.11 = (bf16[288,1152]{1,0:T(8,128)(2,1)}, bf16[288,1152]{1,0:T(8,128)(2,1)}, u32[]{:S(2)}, u32[]{:S(2)}) collective-permute-start(bf16[288,1152]{1,0:T(8,128)(2,1)} %collective-permute-done.7.rest_3_), channel_id=1, source_target_pairs={{0,96},{8,104},{16,112},{24,120},{32,0},{40,8},{48,16},{56,24},{64... | collective-permute-start | bytes 1990664 | tf_op jit(solution)/shard_map/ppermute | solution.py:209
  60.1 14.6 %collective-permute-start.10 = (bf16[288,1152]{1,0:T(8,128)(2,1)}, bf16[288,1152]{1,0:T(8,128)(2,1)}, u32[]{:S(2)}, u32[]{:S(2)}) collective-permute-start(bf16[288,1152]{1,0:T(8,128)(2,1)} %collective-permute-done.7.rest_3_), channel_id=1, source_target_pairs={{0,32},{8,40},{16,48},{24,56},{32,64},{40,72},{48,80},{56,88},{64,... | collective-permute-start | bytes 1990664 | tf_op jit(solution)/shard_map/ppermute | solution.py:209
  60.1 15.2 %collective-permute-start.12 = (bf16[288,1152]{1,0:T(8,128)(2,1)}, bf16[288,1152]{1,0:T(8,128)(2,1)}, u32[]{:S(2)}, u32[]{:S(2)}) collective-permute-start(bf16[288,1152]{1,0:T(8,128)(2,1)} %pad_maximum_fusion), channel_id=1, source_target_pairs={{0,16},{8,24},{16,0},{24,8},{32,48},{40,56},{48,32},{56,40},{64,80... | collective-permute-start | bytes 1990664 | tf_op jit(solution)/shard_map/ppermute | solution.py:209
  125.2 41.0 %collective-permute-start.27 = (bf16[288,1152]{1,0:T(8,128)(2,1)}, bf16[288,1152]{1,0:T(8,128)(2,1)S(1)}, u32[]{:S(2)}, u32[]{:S(2)}) collective-permute-start(bf16[288,1152]{1,0:T(8,128)(2,1)} %get-tuple-element.38), channel_id=1, source_target_pairs={{0,32},{8,40},{16,48},{24,56},{32,64},{40,72},{48,80},{56,88},{64,... | collective-permute-start | bytes 1990664 | tf_op jit(solution)/shard_map/ppermute | solution.py:209
  125.2 41.0 %collective-permute-start.30 = (bf16[288,1152]{1,0:T(8,128)(2,1)}, bf16[288,1152]{1,0:T(8,128)(2,1)S(1)}, u32[]{:S(2)}, u32[]{:S(2)}) collective-permute-start(bf16[288,1152]{1,0:T(8,128)(2,1)} %get-tuple-element.39), channel_id=1, source_target_pairs={{0,16},{8,24},{16,0},{24,8},{32,48},{40,56},{48,32},{56,40},{64,80... | collective-permute-start | bytes 1990664 | tf_op jit(solution)/shard_map/ppermute | solution.py:209
  139.9 20.6 %collective-permute-start.18 = (bf16[288,1152]{1,0:T(8,128)(2,1)S(1)}, bf16[288,1152]{1,0:T(8,128)(2,1)S(1)}, u32[]{:S(2)}, u32[]{:S(2)}) collective-permute-start(bf16[288,1152]{1,0:T(8,128)(2,1)S(1)} %get-tuple-element.41), channel_id=1, source_target_pairs={{0,32},{8,40},{16,48},{24,56},{32,64},{40,72},{48,80},{56,88},{64,... | collective-permute-start | bytes 1990664 | tf_op jit(solution)/shard_map/ppermute | solution.py:209
  140.8 22.1 %collective-permute-start.21 = (bf16[288,1152]{1,0:T(8,128)(2,1)S(1)}, bf16[288,1152]{1,0:T(8,128)(2,1)S(1)}, u32[]{:S(2)}, u32[]{:S(2)}) collective-permute-start(bf16[288,1152]{1,0:T(8,128)(2,1)S(1)} %get-tuple-element.42), channel_id=1, source_target_pairs={{0,16},{8,24},{16,0},{24,8},{32,48},{40,56},{48,32},{56,40},{64,80... | collective-permute-start | bytes 1990664 | tf_op jit(solution)/shard_map/ppermute | solution.py:209
  143.2 19.7 %collective-permute-start.19 = (bf16[288,1152]{1,0:T(8,128)(2,1)S(1)}, bf16[288,1152]{1,0:T(8,128)(2,1)S(1)}, u32[]{:S(2)}, u32[]{:S(2)}) collective-permute-start(bf16[288,1152]{1,0:T(8,128)(2,1)S(1)} %get-tuple-element.43), channel_id=1, source_target_pairs={{0,96},{8,104},{16,112},{24,120},{32,0},{40,8},{48,16},{56,24},{64... | collective-permute-start | bytes 1990664 | tf_op jit(solution)/shard_map/ppermute | solution.py:209
  163.6 17.2 %collective-permute-start.24 = (bf16[144,1152]{1,0:T(8,128)(2,1)S(1)}, bf16[144,1152]{1,0:T(8,128)(2,1)S(1)}, u32[]{:S(2)}, u32[]{:S(2)}) collective-permute-start(bf16[144,1152]{1,0:T(8,128)(2,1)S(1)} %get-tuple-element.51), channel_id=1, source_target_pairs={{0,96},{8,104},{16,112},{24,120},{32,0},{40,8},{48,16},{56,24},{64... | collective-permute-start | bytes 995336 | tf_op jit(solution)/shard_map/ppermute | solution.py:209
  176.8 36.8 %collective-permute-start.29 = (bf16[288,1152]{1,0:T(8,128)(2,1)S(1)}, bf16[288,1152]{1,0:T(8,128)(2,1)S(1)}, u32[]{:S(2)}, u32[]{:S(2)}) collective-permute-start(bf16[288,1152]{1,0:T(8,128)(2,1)S(1)} %get-tuple-element.26), channel_id=1, source_target_pairs={{0,16},{8,24},{16,0},{24,8},{32,48},{40,56},{48,32},{56,40},{64,80... | collective-permute-start | bytes 1990664 | tf_op jit(solution)/shard_map/ppermute | solution.py:209
  177.7 20.7 %collective-permute-start.20 = (bf16[288,1152]{1,0:T(8,128)(2,1)S(1)}, bf16[288,1152]{1,0:T(8,128)(2,1)S(1)}, u32[]{:S(2)}, u32[]{:S(2)}) collective-permute-start(bf16[288,1152]{1,0:T(8,128)(2,1)S(1)} %get-tuple-element.30), channel_id=1, source_target_pairs={{0,16},{8,24},{16,0},{24,8},{32,48},{40,56},{48,32},{56,40},{64,80... | collective-permute-start | bytes 1990664 | tf_op jit(solution)/shard_map/ppermute | solution.py:209
  180.9 21.1 %collective-permute-start.25 = (bf16[288,1152]{1,0:T(8,128)(2,1)S(1)}, bf16[288,1152]{1,0:T(8,128)(2,1)S(1)}, u32[]{:S(2)}, u32[]{:S(2)}) collective-permute-start(bf16[288,1152]{1,0:T(8,128)(2,1)S(1)} %pad_maximum_fusion.2), channel_id=1, source_target_pairs={{0,96},{8,104},{16,112},{24,120},{32,0},{40,8},{48,16},{56,24},{64... | collective-permute-start | bytes 1990664 | tf_op jit(solution)/shard_map/ppermute | solution.py:209
  183.4 18.7 %collective-permute-start.23 = (bf16[288,1152]{1,0:T(8,128)(2,1)S(1)}, bf16[288,1152]{1,0:T(8,128)(2,1)S(1)}, u32[]{:S(2)}, u32[]{:S(2)}) collective-permute-start(bf16[288,1152]{1,0:T(8,128)(2,1)S(1)} %pad_maximum_fusion.1), channel_id=1, source_target_pairs={{0,32},{8,40},{16,48},{24,56},{32,64},{40,72},{48,80},{56,88},{64,... | collective-permute-start | bytes 1990664 | tf_op jit(solution)/shard_map/ppermute | solution.py:209
  188.1 28.2 %collective-permute-start.34 = (bf16[288,1152]{1,0:T(8,128)(2,1)S(1)}, bf16[288,1152]{1,0:T(8,128)(2,1)S(1)}, u32[]{:S(2)}, u32[]{:S(2)}) collective-permute-start(bf16[288,1152]{1,0:T(8,128)(2,1)S(1)} %pad_maximum_fusion.4), channel_id=1, source_target_pairs={{0,96},{8,104},{16,112},{24,120},{32,0},{40,8},{48,16},{56,24},{64... | collective-permute-start | bytes 1990664 | tf_op jit(solution)/shard_map/ppermute | solution.py:209
  198.4 17.9 %collective-permute-start.32 = (bf16[288,1152]{1,0:T(8,128)(2,1)S(1)}, bf16[288,1152]{1,0:T(8,128)(2,1)S(1)}, u32[]{:S(2)}, u32[]{:S(2)}) collective-permute-start(bf16[288,1152]{1,0:T(8,128)(2,1)S(1)} %pad_maximum_fusion.3), channel_id=1, source_target_pairs={{0,32},{8,40},{16,48},{24,56},{32,64},{40,72},{48,80},{56,88},{64,... | collective-permute-start | bytes 1990664 | tf_op jit(solution)/shard_map/ppermute | solution.py:209
  202.5 20.2 %collective-permute-start.26 = (f32[144,1152]{1,0:T(8,128)S(1)}, f32[144,1152]{1,0:T(8,128)S(1)}, u32[]{:S(2)}, u32[]{:S(2)}) collective-permute-start(f32[144,1152]{1,0:T(8,128)S(1)} %get-tuple-element.47), channel_id=1, source_target_pairs={{0,8},{8,0},{16,24},{24,16},{32,40},{40,32},{48,56},{56,48},{64,72... | collective-permute-start | bytes 1990664 | tf_op jit(solution)/shard_map/ppermute | solution.py:209
  (43 other events, 290.6 us)

commit v2 on v0

v2 whole, which is shorter than its diff:
```python
import functools
import math

import jax
import jax.numpy as jnp
from jax import lax
from jax.experimental import pallas as pl
from jax.experimental.pallas import tpu as pltpu
from jax.sharding import PartitionSpec as P

D = 2304
FF = 18432
SEQ = 384
N_DP = 16
N_TENSOR = 8
COST = pl.CostEstimate(flops=1000, bytes_accessed=1000, transcendentals=0)

Z_UP = [(i, (i + 4) % 16) for i in range(16)]
Z_DOWN = [(i, (i + 12) % 16) for i in range(16)]
X_SWAP = [(i, i ^ 2) for i in range(16)]
CORE_SWAP = [(i, i ^ 1) for i in range(16)]
TENSOR_SWAPS = [[(t, t ^ k) for t in range(8)] for k in (4, 1, 3)]


VMEM = pl.BlockSpec(memory_space=pltpu.VMEM)
SMEM = pl.BlockSpec(memory_space=pltpu.SMEM)
HBM = pl.BlockSpec(memory_space=pl.ANY)


def in_vmem(a):
    return pltpu.with_memory_space_constraint(a, pltpu.VMEM)


def in_hbm(a):
    return pltpu.with_memory_space_constraint(a, pltpu.HBM)


def nt(a, b):
    return lax.dot_general(a, b, (((1,), (1,)), ((), ())), preferred_element_type=jnp.float32)


def nn(a, b):
    return lax.dot_general(a, b, (((1,), (0,)), ((), ())), preferred_element_type=jnp.float32)


def tn(a, b):
    return lax.dot_general(a, b, (((0,), (0,)), ((), ())), preferred_element_type=jnp.float32)


def call(kernel, name, in_specs, out_specs, out_shape, scratch=(), mib=28):
    return pl.pallas_call(
        kernel,
        in_specs=in_specs,
        out_specs=out_specs,
        out_shape=out_shape,
        scratch_shapes=list(scratch),
        compiler_params=pltpu.CompilerParams(vmem_limit_bytes=mib << 20),
        cost_estimate=COST,
        name=name,
    )


def rows_of(e):
    return pl.ds(e * SEQ, SEQ)


def chunk(s_ref, j, ref):
    rows = ref.shape[0] // 8
    return pl.ds(pl.multiple_of(s_ref[j] * rows, 32), rows)


def turn(x_ref, dy_ref, dyt_ref, gx_ref, gdy_ref, arrivals):
    for e in range(2):
        arrivals[2 * e].wait()
        x = x_ref[rows_of(e), :]
        gx_ref[e] = nt(x, x)
        arrivals[2 * e + 1].wait()
        dy = dy_ref[rows_of(e), :]
        dyt_ref[:, rows_of(e)] = dy.T
        gdy_ref[e] = nt(dy, dy)


def token_copies(x_hbm, dy_hbm, x_ref, dy_ref, sems):
    pairs = []
    for e in range(2):
        for src, dst in ((x_hbm, x_ref), (dy_hbm, dy_ref)):
            pairs.append((src.at[rows_of(e), :], dst.at[rows_of(e), :]))
    return [pltpu.make_async_copy(src, dst, sems.at[j]) for j, (src, dst) in enumerate(pairs)]


def hidden_norm(gate_ref, up_ref, gdy_ref, hid_ref, vd_ref):
    at = lax.broadcasted_iota(jnp.int32, vd_ref.shape, 0)
    value = jnp.zeros(vd_ref.shape, jnp.float32)
    for e in range(2):
        gate, up = gate_ref[rows_of(e), :].astype(jnp.float32), up_ref[rows_of(e), :].astype(jnp.float32)
        hid = (gate * up).astype(jnp.bfloat16)
        hid_ref[rows_of(e), :] = hid
        value += jnp.where(at == e, jnp.sum(gdy_ref[e] * nt(hid, hid)), 0.0)
    vd_ref[...] = value


def own_kernel(
    s_ref, x_hbm, dy_hbm, gate_hbm, up_hbm, dyt_ref, gx_hbm, gate_ref, hid_ref, vd_ref, sent_ref,
    x_ref, dy_ref, up_ref, gx_ref, gdy_ref, sems,
):
    tok, ff = hid_ref.shape
    tokens = token_copies(x_hbm, dy_hbm, x_ref, dy_ref, sems)
    mine = pl.ds(pl.multiple_of(s_ref[8] * ff, 128), ff)
    other = pl.ds(pl.multiple_of((1 - s_ref[8]) * ff, 128), ff)
    pairs = [
        (gate_hbm.at[:, mine], gate_ref),
        (up_hbm.at[:, mine], up_ref),
        (gate_hbm.at[:, other], sent_ref.at[pl.ds(0, tok), :]),
        (up_hbm.at[:, other], sent_ref.at[pl.ds(tok, tok), :]),
    ]
    columns = [pltpu.make_async_copy(src, dst, sems.at[4 + j]) for j, (src, dst) in enumerate(pairs)]
    for copy in tokens + columns:
        copy.start()
    turn(x_ref, dy_ref, dyt_ref, gx_ref, gdy_ref, tokens)
    keep = pltpu.make_async_copy(gx_ref, gx_hbm, sems.at[8])
    keep.start()
    columns[0].wait()
    columns[1].wait()
    hidden_norm(gate_ref, up_ref, gdy_ref, hid_ref, vd_ref)
    for copy in columns[2:] + [keep]:
        copy.wait()


def prep_own(scalars, x, dy, gate, up, ff):
    tok, width = x.shape
    bf16, f32 = jnp.bfloat16, jnp.float32
    cols = pltpu.VMEM((tok, ff), bf16)
    gram = (2, SEQ, SEQ)
    return call(
        own_kernel,
        "prep_own",
        [SMEM] + [HBM] * 4,
        [VMEM, HBM] + [VMEM] * 4,
        [
            pltpu.VMEM((width, tok), bf16),
            pltpu.HBM(gram, f32),
            cols,
            cols,
            jax.ShapeDtypeStruct((8, 128), f32),
            pltpu.VMEM((2 * tok, ff), bf16),
        ],
        [pltpu.VMEM((tok, width), bf16)] * 2
        + [cols, pltpu.VMEM(gram, f32), pltpu.VMEM(gram, f32), pltpu.SemaphoreType.DMA((9,))],
    )(scalars, *[in_hbm(a) for a in (x, dy, gate, up)])


def other_kernel(x_hbm, dy_hbm, dyt_ref, gx_hbm, gdy_ref, x_ref, dy_ref, gx_ref, sems):
    tokens = token_copies(x_hbm, dy_hbm, x_ref, dy_ref, sems)
    for copy in tokens:
        copy.start()
    turn(x_ref, dy_ref, dyt_ref, gx_ref, gdy_ref, tokens)
    keep = pltpu.make_async_copy(gx_ref, gx_hbm, sems.at[4])
    keep.start()
    keep.wait()


def prep_other(x, dy):
    tok, width = x.shape
    bf16, f32 = jnp.bfloat16, jnp.float32
    gram = (2, SEQ, SEQ)
    return call(
        other_kernel,
        "prep_other",
        [HBM] * 2,
        [VMEM, HBM, VMEM],
        [pltpu.VMEM((width, tok), bf16), pltpu.HBM(gram, f32), pltpu.VMEM(gram, f32)],
        [pltpu.VMEM((tok, width), bf16)] * 2 + [pltpu.VMEM(gram, f32), pltpu.SemaphoreType.DMA((5,))],
    )(in_hbm(x), in_hbm(dy))


def hidden_kernel(gu_ref, gdy_ref, hid_ref, vd_ref):
    tok = hid_ref.shape[0]
    hidden_norm(gu_ref.at[pl.ds(0, tok), :], gu_ref.at[pl.ds(tok, tok), :], gdy_ref, hid_ref, vd_ref)


def hidden_other(gu, gdy):
    tok, ff = gu.shape[0] // 2, gu.shape[1]
    return call(
        hidden_kernel,
        "hidden_other",
        [VMEM] * 2,
        [VMEM] * 2,
        [pltpu.VMEM((tok, ff), jnp.bfloat16), jax.ShapeDtypeStruct((8, 128), jnp.float32)],
    )(in_vmem(gu), in_vmem(gdy))


def halves_kernel(a_ref, b_ref, top_ref, bottom_ref, sems):
    half = top_ref.shape[0]
    copies = [
        pltpu.make_async_copy(a_ref.at[pl.ds(0, half), :], top_ref, sems.at[0]),
        pltpu.make_async_copy(b_ref.at[pl.ds(half, half), :], bottom_ref, sems.at[1]),
    ]
    for copy in copies:
        copy.start()
    for copy in copies:
        copy.wait()


def halves(a, b):
    half = pltpu.VMEM((a.shape[0] // 2, a.shape[1]), a.dtype)
    return call(halves_kernel, "halves", [HBM] * 2, [VMEM] * 2, [half, half], [pltpu.SemaphoreType.DMA((2,))])(
        in_hbm(a), in_hbm(b)
    )


def fetch(pieces, w_ref, sems):
    copies, at = [], 0
    for j, piece in enumerate(pieces):
        n = piece.shape[0]
        copies.append(pltpu.make_async_copy(piece, w_ref.at[pl.ds(at, n), :], sems.at[j]))
        at += n
    for copy in copies:
        copy.start()
    for copy in copies:
        copy.wait()


def chunks_of(s_ref, first, n, ref, columns):
    return jnp.concatenate([ref[chunk(s_ref, j, ref), columns] for j in range(first, first + n)])


def near_kernel(n, s_ref, dyt_ref, *rest):
    pieces, (out_ref, w_ref, sems) = rest[:-3], rest[-3:]
    fetch(pieces, w_ref, sems)
    for e in range(2):
        out_ref[rows_of(e), :] = tn(chunks_of(s_ref, 0, n, dyt_ref, rows_of(e)), w_ref[...])


def near(scalars, dyt, pieces, name):
    width, tok = dyt.shape
    ff, n = pieces[0].shape[1], len(pieces)
    return call(
        functools.partial(near_kernel, n),
        name,
        [SMEM, VMEM] + [HBM] * n,
        VMEM,
        pltpu.VMEM((tok, ff), jnp.float32),
        [pltpu.VMEM((width // 8 * n, ff), jnp.bfloat16), pltpu.SemaphoreType.DMA((n,))],
    )(scalars, in_vmem(dyt), *[in_hbm(a) for a in pieces])


def act_kernel(near_counts, s_ref, dya, dyb, na, nb, ga, gb, gxa, gxb, vda, vdb, *rest):
    pieces, (act_hbm_a, act_hbm_b, v_ref, w_ref, act_ref, sems) = rest[:-6], rest[-6:]
    fetch(pieces, w_ref, sems)
    at = lax.broadcasted_iota(jnp.int32, v_ref.shape, 0)
    value = vda[...] + pltpu.roll(vdb[...], 2, 0)
    copies = []
    depth = w_ref.shape[0]
    for half, (n, dyt, near_ref, gate, gx, act_hbm) in enumerate(
        zip(near_counts, (dya, dyb), (na, nb), (ga, gb), (gxa, gxb), (act_hbm_a, act_hbm_b))
    ):
        below = depth - dyt.shape[0] // 8 * (8 - n)
        w = w_ref[below:, :]
        for e in range(2):
            grad = near_ref[rows_of(e), :] + tn(chunks_of(s_ref, n, 8 - n, dyt, rows_of(e)), w)
            act = (grad * gate[rows_of(e), :].astype(jnp.float32)).astype(jnp.bfloat16)
            k = 2 * half + e
            act_ref[rows_of(k), :] = act
            copies.append(pltpu.make_async_copy(act_ref.at[rows_of(k), :], act_hbm.at[rows_of(e), :], sems.at[8 + k]))
            copies[-1].start()
            value += jnp.where(at == k, jnp.sum(gx[e] * nt(act, act)), 0.0)
    v_ref[...] = value
    for copy in copies:
        copy.wait()


def act_grads(near_counts, scalars, dyt_a, dyt_b, near_a, near_b, gate_a, gate_b, gx_a, gx_b, vd_a, vd_b, pieces):
    width, tok = dyt_a.shape
    ff = near_a.shape[1]
    grads = pltpu.HBM((tok, ff), jnp.bfloat16)
    args = [in_vmem(a) for a in (dyt_a, dyt_b, near_a, near_b, gate_a, gate_b, gx_a, gx_b)]
    return call(
        functools.partial(act_kernel, near_counts),
        "act_grads",
        [SMEM] + [VMEM] * 10 + [HBM] * len(pieces),
        [HBM, HBM, VMEM],
        [grads, grads, jax.ShapeDtypeStruct((8, 128), jnp.float32)],
        [
            pltpu.VMEM((width // 8 * (8 - min(near_counts)), ff), jnp.bfloat16),
            pltpu.VMEM((2 * tok, ff), jnp.bfloat16),
            pltpu.SemaphoreType.DMA((12,)),
        ],
    )(scalars, *args, vd_a, vd_b, *[in_hbm(a) for a in pieces])


def clip_rows(p_ref, q_ref, ra_ref, rb_ref, sa_ref, sb_ref):
    bound = 4.0 * math.sqrt(D * FF)
    sq_norm = jnp.maximum(p_ref[...] + q_ref[...], 0.0)
    clip = bound / jnp.maximum(jnp.sqrt(sq_norm), bound)
    for e in range(2):
        at = rows_of(e)
        sa_ref[at, :] = (ra_ref[at, :].astype(jnp.float32) * clip[e : e + 1, :1]).astype(jnp.bfloat16)
        sb_ref[at, :] = (rb_ref[at, :].astype(jnp.float32) * clip[e + 2 : e + 3, :1]).astype(jnp.bfloat16)


def share_kernel(s_ref, p_ref, q_ref, la_ref, lb_ref, ra_ref, rb_ref, *rest):
    n = s_ref.shape[0]
    outs, (sa_ref, sb_ref) = rest[:n], rest[n:]
    clip_rows(p_ref, q_ref, ra_ref, rb_ref, sa_ref, sb_ref)
    for j, out in enumerate(outs):
        at = chunk(s_ref, j, la_ref)
        out[...] = (nn(la_ref[at, :], sa_ref[...]) + nn(lb_ref[at, :], sb_ref[...])).astype(out.dtype)


def shares(scalars, p, q, lhs_a, lhs_b, rhs_a, rhs_b, dtypes, name):
    tok, ff = rhs_a.shape
    n, rows = scalars.shape[0], lhs_a.shape[0] // 8
    return call(
        share_kernel,
        name,
        [SMEM] + [VMEM] * 6,
        [VMEM] * n,
        [jax.ShapeDtypeStruct((rows, ff), dtype) for dtype in dtypes],
        [pltpu.VMEM((tok, ff), jnp.bfloat16)] * 2,
    )(scalars, p, q, *[in_vmem(a) for a in (lhs_a, lhs_b, rhs_a, rhs_b)])


def all_shares_kernel(dtypes, s_ref, p_ref, q_ref, xa_hbm, xb_hbm, ra_hbm, rb_hbm, *rest):
    outs, (xa_ref, xb_ref, xta_ref, xtb_ref, sa_ref, sb_ref, narrow_ref, wide_ref, sems) = rest[:8], rest[8:]
    copies = [
        pltpu.make_async_copy(src, dst, sems.at[j])
        for j, (src, dst) in enumerate(((xa_hbm, xa_ref), (ra_hbm, sa_ref), (rb_hbm, sb_ref), (xb_hbm, xb_ref)))
    ]
    copies[0].start()
    copies[1].start()
    copies[0].wait()
    copies[2].start()
    copies[3].start()
    xta_ref[...] = xa_ref[...].T
    copies[1].wait()
    copies[2].wait()
    clip_rows(p_ref, q_ref, sa_ref, sb_ref, sa_ref, sb_ref)
    copies[3].wait()
    xtb_ref[...] = xb_ref[...].T
    stores = {jnp.float32: [], jnp.bfloat16: []}
    for j, (dtype, out) in enumerate(zip(dtypes, outs)):
        at = chunk(s_ref, j, xta_ref)
        earlier = stores[dtype]
        held = (wide_ref if dtype == jnp.float32 else narrow_ref).at[len(earlier) % 2]
        if len(earlier) >= 2:
            earlier[-2].wait()
        held[...] = (nn(xta_ref[at, :], sa_ref[...]) + nn(xtb_ref[at, :], sb_ref[...])).astype(dtype)
        earlier.append(pltpu.make_async_copy(held, out, sems.at[4 + j]))
        earlier[-1].start()
    for earlier in stores.values():
        for copy in earlier[-2:]:
            copy.wait()


def all_shares(scalars, p, q, x_a, x_b, rhs_a, rhs_b, dtypes, name):
    tok, ff = rhs_a.shape
    width = x_a.shape[1]
    rows = width // 8
    turned = pltpu.VMEM((width, tok), jnp.bfloat16)
    cols = pltpu.VMEM((tok, ff), jnp.bfloat16)
    return call(
        functools.partial(all_shares_kernel, dtypes),
        name,
        [SMEM, VMEM, VMEM] + [HBM] * 4,
        [HBM] * 8,
        [pltpu.HBM((rows, ff), dtype) for dtype in dtypes],
        [pltpu.VMEM((tok, width), jnp.bfloat16)] * 2
        + [turned, turned, cols, cols]
        + [pltpu.VMEM((2, rows, ff), jnp.bfloat16), pltpu.VMEM((2, rows, ff), jnp.float32)]
        + [pltpu.SemaphoreType.DMA((12,))],
    )(scalars, p, q, *[in_hbm(a) for a in (x_a, x_b, rhs_a, rhs_b)])


def take(hbm_refs, refs, sems):
    copies = [pltpu.make_async_copy(src, dst, sems.at[j]) for j, (src, dst) in enumerate(zip(hbm_refs, refs))]
    for copy in copies:
        copy.start()
    for copy in copies:
        copy.wait()


def join_kernel(staged, *refs):
    ins, (s4_ref, top_ref, bottom_ref), (*held, sems) = refs[:5], refs[5:8], refs[8:]
    f32, bf16 = jnp.float32, jnp.bfloat16
    take(ins if staged else ins[2:], held, sems)
    m4_ref, m3_ref, r2p_ref, r2m_ref, r1_ref = held if staged else list(ins[:2]) + held
    half = top_ref.shape[0]
    s3 = (m3_ref[...] + r1_ref[...].astype(f32)).astype(bf16)
    top_ref[...] = s3[:half]
    bottom_ref[...] = s3[half:]
    s4_ref[...] = (m4_ref[...] + r2p_ref[...].astype(f32) + r2m_ref[...].astype(f32)).astype(bf16)


def join(staged, m4, m3, r2p, r2m, r1, name):
    rows, ff = m4.shape
    bf16 = jnp.bfloat16
    half = jax.ShapeDtypeStruct((rows // 2, ff), bf16)
    arrays = [m4, m3, r2p, r2m, r1]
    held = arrays if staged else arrays[2:]
    return call(
        functools.partial(join_kernel, staged),
        name,
        [HBM if staged else VMEM] * 2 + [HBM] * 3,
        [VMEM] * 3,
        [jax.ShapeDtypeStruct((rows, ff), bf16), half, half],
        [pltpu.VMEM((rows, ff), a.dtype) for a in held] + [pltpu.SemaphoreType.DMA((len(held),))],
    )(*(arrays[: 5 - len(held)] + [in_hbm(a) for a in held]))


def last_hop_kernel(*refs):
    hbm, (sp_ref, sm_ref), (mp_ref, mm_ref, rp_ref, rm_ref, sems) = refs[:4], refs[4:6], refs[6:]
    f32, bf16 = jnp.float32, jnp.bfloat16
    take(hbm, (mp_ref, mm_ref, rp_ref, rm_ref), sems)
    half = rp_ref.shape[0]
    upper, lower = pl.ds(0, half), pl.ds(half, half)
    sp_ref[upper, :] = (mp_ref[upper, :].astype(f32) + rp_ref[...].astype(f32)).astype(bf16)
    sp_ref[lower, :] = mp_ref[lower, :].astype(bf16)
    sm_ref[upper, :] = mm_ref[upper, :].astype(bf16)
    sm_ref[lower, :] = (mm_ref[lower, :].astype(f32) + rm_ref[...].astype(f32)).astype(bf16)


def last_hop(mp, mm, rp, rm, name):
    out = jax.ShapeDtypeStruct(mp.shape, jnp.bfloat16)
    arrays = (mp, mm, rp, rm)
    return call(
        last_hop_kernel,
        name,
        [HBM] * 4,
        [VMEM] * 2,
        [out, out],
        [pltpu.VMEM(a.shape, a.dtype) for a in arrays] + [pltpu.SemaphoreType.DMA((4,))],
    )(*[in_hbm(a) for a in arrays])


def total_kernel(s_ref, *refs):
    (down, up), (kept_d, kept_u, other_ref) = (refs[:4], refs[4:8]), refs[8:]
    half = kept_d.shape[0]
    mine = pl.ds(pl.multiple_of(s_ref[8] * half, 16), half)
    others = pl.ds(pl.multiple_of((1 - s_ref[8]) * half, 16), half)
    for (m, *got), kept, at in ((down, kept_d, 0), (up, kept_u, half)):
        for src, dst in ((mine, kept), (others, other_ref.at[pl.ds(at, half), :])):
            got4, gotp, gotm = [r[src, :].astype(jnp.float32) for r in got]
            dst[...] = (m[src, :] + got4 + gotp + gotm).astype(dst.dtype)


def totals(scalars, down, up):
    rows, ff = down[0].shape
    half = jax.ShapeDtypeStruct((rows // 2, ff), jnp.float32)
    return call(
        total_kernel,
        "totals",
        [SMEM] + [VMEM] * 8,
        [VMEM] * 3,
        [half, half, jax.ShapeDtypeStruct((rows, ff), jnp.bfloat16)],
    )(scalars, *down, *up)


def update_kernel(s_ref, kept_d, kept_u, other_ref, noise_d, noise_u, out_d, out_u):
    half, ff = kept_d.shape
    mine = pl.ds(pl.multiple_of(s_ref[8] * ff, 128), ff)
    others = pl.ds(pl.multiple_of((1 - s_ref[8]) * ff, 128), ff)
    for at, kept, noise, out in ((0, kept_d, noise_d, out_d), (half, kept_u, noise_u, out_u)):
        out[:, mine] = (kept[...] + noise[:, mine]) * (1.0 / (2 * N_DP))
        out[:, others] = (other_ref[pl.ds(at, half), :].astype(jnp.float32) + noise[:, others]) * (1.0 / (2 * N_DP))


def updates(scalars, kept_d, kept_u, other, noise_d, noise_u):
    out = jax.ShapeDtypeStruct(noise_d.shape, jnp.float32)
    return call(update_kernel, "updates", [SMEM] + [VMEM] * 5, [VMEM] * 2, [out, out])(
        scalars, kept_d, kept_u, other, noise_d, noise_u
    )


def after(values, *earlier):
    return lax.optimization_barrier((tuple(values),) + earlier)[0]


def on_device(inputs, up_pre, gate_act, out_grad, down_weight, noise_up, noise_down):
    ff = up_pre.shape[1] // 2
    own_rows = down_weight.shape[0]
    me = lax.axis_index("dp")
    core, x, z = me % 2, (me // 2) % 2, me // 4

    def chip(dz, dx):
        return ((z + dz) % 4) * 2 + ((x + dx) % 2)

    def half_cols(a, which):
        return lax.dynamic_slice(a, (0, which * ff), (a.shape[0], ff))

    def go(a, perm):
        return lax.ppermute(a, "dp", perm)

    near_chips = [chip(0, 0), chip(3, 0), chip(1, 0), chip(0, 1), chip(2, 0)]
    far_chips = [chip(3, 1), chip(1, 1), chip(2, 1)]
    scalars = jnp.stack(near_chips + far_chips + [core]).astype(jnp.int32)

    w_mine = half_cols(down_weight, core)
    w_other = go(half_cols(down_weight, 1 - core), CORE_SWAP)
    own = jnp.where(core == 0, jnp.concatenate([w_mine, w_other]), jnp.concatenate([w_other, w_mine]))
    w_zm = go(own, Z_UP)
    w_zp = go(own, Z_DOWN)
    w_x = go(own, X_SWAP)

    dy_src, x_src = after([out_grad, inputs], own)
    dy_b = go(dy_src, CORE_SWAP)
    x_b = go(x_src, CORE_SWAP)
    x_own, dy_own = after([inputs, out_grad], own)
    dyt_a, gx_a, gate_a, hid_a, vd_a, gu_send = prep_own(scalars, x_own, dy_own, gate_act, up_pre, ff)

    x_b, dy_b = after([x_b, dy_b], vd_a)
    dyt_b, gx_b, gdy_b = prep_other(x_b, dy_b)

    w_zm, w_zp, w_x, gu_send = after([w_zm, w_zp, w_x, gu_send], dyt_b)
    up_half, down_half = halves(w_zm, w_zp)
    w_z2_top = go(up_half, Z_UP)
    w_z2_bot = go(down_half, Z_DOWN)
    gu_b = go(gu_send, CORE_SWAP)
    w_x = after([w_x], up_half)[0]
    w_zm_x = go(w_x, Z_UP)
    w_zp_x = go(w_x, Z_DOWN)
    near_a = near(scalars, after([dyt_a], up_half)[0], [own, w_zm, w_zp, w_x], "near_own")
    w_z2_top, w_z2_bot = after([w_z2_top, w_z2_bot], near_a)
    w_z2 = jnp.concatenate([w_z2_top, w_z2_bot])
    w_z2_x = go(w_z2, X_SWAP)
    hid_b, vd_b = hidden_other(after([gu_b], w_z2)[0], gdy_b)
    near_b = near(scalars, after([dyt_b], hid_b)[0], [own, w_zm, w_zp, w_x, w_z2], "near_other")
    w_zm_x, w_zp_x, w_z2_x = after([w_zm_x, w_zp_x, w_z2_x], near_b, vd_b)
    far_pieces = [w_z2, w_zm_x, w_zp_x, w_z2_x]
    act_a, act_b, part = act_grads(
        (4, 5), scalars, dyt_a, dyt_b, near_a, near_b, gate_a, gu_b, gx_a, gx_b, vd_a, vd_b, far_pieces
    )

    got = go(part, CORE_SWAP)
    part = part + jnp.concatenate([got[2:4], got[0:2], got[4:]])
    for swap in TENSOR_SWAPS[:2]:
        part = part + lax.ppermute(part, "tensor", swap)
    rest = lax.ppermute(part, "tensor", TENSOR_SWAPS[2])

    early_chips = [chip(1, 1), chip(3, 1), chip(2, 1)]
    late_chips = [chip(0, 1), chip(2, 0), chip(1, 0), chip(3, 0), chip(0, 0)]
    early = jnp.stack(early_chips).astype(jnp.int32)
    late = jnp.stack(late_chips).astype(jnp.int32)
    every = jnp.concatenate([early, late])

    f32, bf16 = jnp.float32, jnp.bfloat16
    kinds = [f32, f32, bf16, bf16, f32]
    down_args = (part, rest, dyt_a, dyt_b, hid_a, hid_b)
    down_p, down_m, down_x = shares(early, *down_args, [bf16] * 3, "down_first")
    d2p, d2m, d1 = go(down_p, Z_UP), go(down_m, Z_DOWN), go(down_x, X_SWAP)
    act_a, act_b = after([act_a, act_b], down_x)
    up_p, up_m, up_x, up4, up3, up5p, up5m, up_own = all_shares(
        every, part, rest, inputs, x_b, act_a, act_b, [bf16] * 3 + kinds, "up_all"
    )
    d2p, d2m, d1 = after([d2p, d2m, d1], up_x)
    u2p, u2m, u1 = go(up_p, Z_UP), go(up_m, Z_DOWN), go(up_x, X_SWAP)
    late2 = after([late], d2p, d2m)[0]
    down4, down3, down5p, down5m, down_own = shares(late2, *down_args, kinds, "down_later")
    s4d, s3dt, s3db = join(False, down4, down3, d2p, d2m, d1, "down_join")
    d3p, d3m, d4 = go(s3dt, Z_UP), go(s3db, Z_DOWN), go(s4d, X_SWAP)
    u2p, u2m, u1 = after([u2p, u2m, u1], s3dt)
    s4u, s3ut, s3ub = join(True, up4, up3, u2p, u2m, u1, "up_join")
    u3p, u3m, u4 = go(s3ut, Z_UP), go(s3ub, Z_DOWN), go(s4u, X_SWAP)
    d3p, d3m, d4 = after([d3p, d3m, d4], s3ut)
    d3p, d3m = after([d3p, d3m], d4)
    s5dp, s5dm = last_hop(down5p, down5m, d3p, d3m, "down_last")
    d5p, d5m = go(s5dp, Z_UP), go(s5dm, Z_DOWN)
    u3p, u3m = after([u3p, u3m], s5dp)
    s5up, s5um = last_hop(up5p, up5m, u3p, u3m, "up_last")
    u5p, u5m = go(s5up, Z_UP), go(s5um, Z_DOWN)

    d5p, d5m, u4 = after([d5p, d5m, u4], s5up)
    kept_d, kept_u, other = totals(scalars, (down_own, d4, d5p, d5m), (up_own, u4, u5p, u5m))
    other = go(other, CORE_SWAP)
    down_update, up_update = updates(scalars, kept_d, kept_u, other, noise_down, noise_up)
    return (up_update, down_update)


def solution(mesh):
    in_specs = (
        P("dp", None),
        P("dp", "tensor"),
        P("dp", "tensor"),
        P("dp", None),
        P("dp", "tensor"),
        P("dp", "tensor"),
        P("dp", "tensor"),
    )
    out_specs = (P("dp", "tensor"), P("dp", "tensor"))
    return jax.shard_map(
        on_device, mesh=mesh, in_specs=in_specs, out_specs=out_specs, check_vma=False
    )
```

time: 448 us -> 196 us (0.44)
  waiting for transfers between devices: 265 us -> 43.3 us
  Pallas kernels: 0 us -> 80.2 us
  starting transfers between devices: 0.12 us -> 59.6 us
  matrix products: 58 us -> 0 us
  other arithmetic: 49.9 us -> 1.12 us
  local copies, waits for them, and re-layouts: 44.9 us -> 7.38 us
  blocking collectives: 14.9 us -> 0 us
  between operations: 13.8 us -> 1.22 us
    unnamed x5 -> x0, waiting for transfers between devices: 203 us -> none
    pallas_call x0 -> x16, Pallas kernels: none -> 80.2 us  [the longest x1 18.4 us: all_shares(): call(functools.partial(all_shares_kernel, dtypes), name, [SMEM, VMEM, VME...]
    all_gather x1 -> x0, waiting for transfers between devices: 62.7 us -> none  [on_device(): lax.all_gather(down_weight, 'dp', axis=0, tiled=True)]
    ppermute x0 -> x33, starting transfers between devices: none -> 59.6 us  [the longest x30 55.2 us: go(): return lax.ppermute(a, 'dp', perm)]
    dot_general x3 -> x0, matrix products: 58 us -> none  [the longest x1 23.8 us: on_device(): jnp.einsum('esr,esf->erf', x_ex, act_ex, preferred_element_type=jnp.float32)]
    ppermute x0 -> x33, waiting for transfers between devices: none -> 43.3 us  [the longest x30 39.1 us: go(): return lax.ppermute(a, 'dp', perm)]
    unnamed x12 -> x43, local copies, waits for them, and re-layouts: 44.9 us -> 5.96 us
    reduce_sum x1 -> x0, other arithmetic: 38.6 us -> none  [on_device(): jnp.sum(scale[:, None, None] * rows, axis=0).astype(jnp.bfloat16)]
  transfers between devices with their start and end apart: 3 -> 33, of which waited for: 3 -> 16; matrix products, arithmetic and copies ran while one was open for 12% -> 0% of each run, Pallas kernels for 0% -> 32%
where the time goes in v2:
time: 196 us; the launch traced here: 193 us
  Pallas kernels  80.2 us (41%)
  starting transfers between devices  59.6 us (30%)
  waiting for transfers between devices  43.3 us (22%)
  local copies, waits for them, and re-layouts  7.38 us (4%)
    ppermute x30, starting transfers between devices, go(): return lax.ppermute(a, 'dp', perm)  55.2 us
    ppermute x30, waiting for transfers between devices, go(): return lax.ppermute(a, 'dp', perm)  39.1 us
    pallas_call x1, Pallas kernels, all_shares(): call(functools.partial(all_shares_kernel, dtypes), name, [SMEM, VMEM, VME...  18.4 us
    pallas_call x2, Pallas kernels, shares(): call(share_kernel, name, [SMEM] + [VMEM] * 6, [VMEM] * n, [jax.ShapeDtype...  11.7 us
    pallas_call x2, Pallas kernels, near(): call(functools.partial(near_kernel, n), name, [SMEM, VMEM] + [HBM] * n, V...  11.4 us
    pallas_call x1, Pallas kernels, act_grads(): call(functools.partial(act_kernel, near_counts), 'act_grads', [SMEM] + [V...  9.76 us
    pallas_call x1, Pallas kernels, prep_own(): call(own_kernel, 'prep_own', [SMEM] + [HBM] * 4, [VMEM, HBM] + [VMEM] * 4...  7.96 us
    pallas_call x1, Pallas kernels, prep_other(): call(other_kernel, 'prep_other', [HBM] * 2, [VMEM, HBM, VMEM], [pltpu.VME...  6.56 us
  transfers between devices with their start and end apart: 33, of which 16 were waited for; matrix products, arithmetic and copies ran while one was open for 0% of the time, Pallas kernels for 32%

profile of v2, /device:TPU:1, one launch (start us, length us, event | category | flops | bytes accessed | tf_op | source)
XLA Modules:
  0.0 192.8 jit_solution(14733903010708382208)
XLA Ops:
  6.1 2.8 %collective-permute-start.5 = (bf16[288,1152]{1,0:T(8,128)(2,1)}, bf16[288,1152]{1,0:T(8,128)(2,1)}, u32[]{:S(2)}, u32[]{:S(2)}) collective-permute-start(bf16[288,1152]{1,0:T(8,128)(2,1)} %maximum_select_fusion.rest_0_), channel_id=1, source_target_pairs={{0,16},{8,24},{16,0},{24,8},{32,48},{40,56},{48,32},{56,40},{64,80... | collective-permute-start | bytes 1990664 | tf_op jit(solution)/shard_map/ppermute | solution.py:491
  8.9 3.8 %collective-permute-start.4 = (bf16[288,1152]{1,0:T(8,128)(2,1)}, bf16[288,1152]{1,0:T(8,128)(2,1)}, u32[]{:S(2)}, u32[]{:S(2)}) collective-permute-start(bf16[288,1152]{1,0:T(8,128)(2,1)} %maximum_select_fusion.rest_0_), channel_id=1, source_target_pairs={{0,96},{8,104},{16,112},{24,120},{32,0},{40,8},{48,16},{56,24},{64... | collective-permute-start | bytes 1990664 | tf_op jit(solution)/shard_map/ppermute | solution.py:491
  12.8 8.0 %prep_own.1 = (bf16[2304,768]{1,0:T(8,128)(2,1)S(1)}, f32[2,384,384]{2,1,0:T(8,128)}, bf16[768,1152]{1,0:T(8,128)(2,1)S(1)}, bf16[768,1152]{1,0:T(8,128)(2,1)S(1...) custom-call(s32[9]{0:T(128)S(1)} %stack.53.s_ref, bf16[768,2304]{1,0:T(8,128)(2,1)} %xa_hbm.1, ...), custom_call_target="tpu_custom_call" | custom-call | flops 1000 | bytes 1000 | tf_op jit(solution)/shard_map/prep_own/pallas_call | solution.py:134
  20.8 6.6 %prep_other.1 = (bf16[2304,768]{1,0:T(8,128)(2,1)S(1)}, f32[2,384,384]{2,1,0:T(8,128)}, f32[2,384,384]{2,1,0:T(8,128)S(1)}) custom-call(bf16[768,2304]{1,0:T(8,128)(2,1)} %collective-permute-done.1.x_hbm.xb_hbm, bf16[768,2304]{1,0:T(8,128)(2,1)} %collective-permute-done.2.dy_hbm), custom_call_target="tpu_custom_call" | custom-call | flops 1000 | bytes 1000 | tf_op jit(solution)/shard_map/prep_other/pallas_call | solution.py:166
  35.5 11.4 %collective-permute-start.9 = (bf16[288,1152]{1,0:T(8,128)(2,1)}, bf16[288,1152]{1,0:T(8,128)(2,1)S(1)}, u32[]{:S(2)}, u32[]{:S(2)}) collective-permute-start(bf16[288,1152]{1,0:T(8,128)(2,1)} %collective-permute-done.5.rest_3_), channel_id=1, source_target_pairs={{0,32},{8,40},{16,48},{24,56},{32,64},{40,72},{48,80},{56,88},{64,... | collective-permute-start | bytes 1990664 | tf_op jit(solution)/shard_map/ppermute | solution.py:491
  46.9 5.0 %near_own.1.na = f32[768,1152]{1,0:T(8,128)S(1)} custom-call(s32[9]{0:T(128)S(1)} %stack.53.s_ref, bf16[2304,768]{1,0:T(8,128)(2,1)S(1)} %get-tuple-element.100.dyt_ref.dya.la_ref, bf16[288,1152]{1,0:T(8,128)(2,1)} %maximum_select_fusion.rest_0_, bf16[288,1152]{1,0:T(8,128)(2,1)} %collective-permute-done.3.a_ref.rest_1_, ...), custom_call_target="tpu_custom_call" | custom-call | flops 1000 | bytes 1000 | tf_op jit(solution)/shard_map/near_own/pallas_call | solution.py:237
  53.7 6.5 %near_other.1.nb = f32[768,1152]{1,0:T(8,128)S(1)} custom-call(s32[9]{0:T(128)S(1)} %stack.53.s_ref, bf16[2304,768]{1,0:T(8,128)(2,1)S(1)} %get-tuple-element.110.dyt_ref.dyb.lb_ref, bf16[288,1152]{1,0:T(8,128)(2,1)} %maximum_select_fusion.rest_0_, bf16[288,1152]{1,0:T(8,128)(2,1)} %collective-permute-done.3.a_ref.rest_1_, ...), custom_call_target="tpu_custom_call" | custom-call | flops 1000 | bytes 1000 | tf_op jit(solution)/shard_map/near_other/pallas_call | solution.py:237
  60.2 3.0 %collective-permute-done.9.rest_1_ = bf16[288,1152]{1,0:T(8,128)(2,1)S(1)} collective-permute-done((bf16[288,1152]{1,0:T(8,128)(2,1)}, bf16[288,1152]{1,0:T(8,128)(2,1)S(1)}, u32[]{:S(2)}, u32[]{:S(2)}) %collective-permute-start.9) | collective-permute-done | bytes 663584 | tf_op jit(solution)/shard_map/ppermute | solution.py:491
  63.3 5.5 %collective-permute-done.11.rest_3_ = bf16[288,1152]{1,0:T(8,128)(2,1)S(1)} collective-permute-done((bf16[288,1152]{1,0:T(8,128)(2,1)S(1)}, bf16[288,1152]{1,0:T(8,128)(2,1)S(1)}, u32[]{:S(2)}, u32[]{:S(2)}) %collective-permute-start.11) | collective-permute-done | bytes 663584 | tf_op jit(solution)/shard_map/ppermute | solution.py:491
  69.6 9.8 %act_grads.1 = (bf16[768,1152]{1,0:T(8,128)(2,1)}, bf16[768,1152]{1,0:T(8,128)(2,1)}, f32[8,128]{1,0:T(8,128)S(1)}) custom-call(s32[9]{0:T(128)S(1)} %stack.53.s_ref, bf16[2304,768]{1,0:T(8,128)(2,1)S(1)} %get-tuple-element.100.dyt_ref.dya.la_ref, bf16[2304,768]{1,0:T(8,128)(2,1)S(1)} %get-tuple-element.110.dyt_ref.dyb.lb_ref, f32[768,1152]{1,0:T(8,128)S(1)} %near_own.1.na, ...), custom_call_target="tpu_custom_call" | custom-call | flops 1000 | bytes 1000 | tf_op jit(solution)/shard_map/act_grads/pallas_call | solution.py:277
  87.4 2.7 %collective-permute-start.15 = (f32[8,128]{1,0:T(8,128)S(1)}, f32[8,128]{1,0:T(8,128)S(1)}, u32[]{:S(2)}, u32[]{:S(2)}) collective-permute-start(f32[8,128]{1,0:T(8,128)S(1)} %add.152.p_ref), channel_id=1, source_target_pairs={{0,3},{1,2},{2,1},{3,0},{4,7},{5,6},{6,5},{7,4},{8,11},{9,10},{10,... | collective-permute-start | bytes 12296 | tf_op jit(solution)/shard_map/ppermute | solution.py:537
  91.1 5.2 %down_first.1 = (bf16[288,1152]{1,0:T(8,128)(2,1)}, bf16[288,1152]{1,0:T(8,128)(2,1)}, bf16[288,1152]{1,0:T(8,128)(2,1)}) custom-call(s32[3]{0:T(128)S(1)} %pad_add_fusion.s_ref, f32[8,128]{1,0:T(8,128)S(1)} %add.152.p_ref, f32[8,128]{1,0:T(8,128)S(1)} %collective-permute-done.15.q_ref, bf16[2304,768]{1,0:T(8,128)(2,1)S(1)} %get-tuple-element.100.dyt_ref.dya.la_ref, ...), custom_call_target="tpu_custom_call" | custom-call | flops 1000 | bytes 1000 | tf_op jit(solution)/shard_map/down_first/pallas_call | solution.py:313
  96.3 2.7 %collective-permute-start.17 = (bf16[288,1152]{1,0:T(8,128)(2,1)}, bf16[288,1152]{1,0:T(8,128)(2,1)}, u32[]{:S(2)}, u32[]{:S(2)}) collective-permute-start(bf16[288,1152]{1,0:T(8,128)(2,1)} %get-tuple-element.121), channel_id=1, source_target_pairs={{0,96},{8,104},{16,112},{24,120},{32,0},{40,8},{48,16},{56,24},{64... | collective-permute-start | bytes 1990664 | tf_op jit(solution)/shard_map/ppermute | solution.py:491
  100.0 18.4 %up_all.1 = (bf16[288,1152]{1,0:T(8,128)(2,1)}, bf16[288,1152]{1,0:T(8,128)(2,1)}, bf16[288,1152]{1,0:T(8,128)(2,1)}, f32[288,1152]{1,0:T(8,128)}, f32[288,1152]...) custom-call(s32[8]{0:T(128)S(1)} %concatenate.20.s_ref, ...), custom_call_target="tpu_custom_call" | custom-call | flops 1000 | bytes 1000 | tf_op jit(solution)/shard_map/up_all/pallas_call | solution.py:361
  118.5 2.7 %collective-permute-start.23 = (bf16[288,1152]{1,0:T(8,128)(2,1)}, bf16[288,1152]{1,0:T(8,128)(2,1)}, u32[]{:S(2)}, u32[]{:S(2)}) collective-permute-start(bf16[288,1152]{1,0:T(8,128)(2,1)} %get-tuple-element.141), channel_id=1, source_target_pairs={{0,96},{8,104},{16,112},{24,120},{32,0},{40,8},{48,16},{56,24},{64... | collective-permute-start | bytes 1990664 | tf_op jit(solution)/shard_map/ppermute | solution.py:491
  121.2 2.5 %collective-permute-start.24 = (bf16[288,1152]{1,0:T(8,128)(2,1)}, bf16[288,1152]{1,0:T(8,128)(2,1)}, u32[]{:S(2)}, u32[]{:S(2)}) collective-permute-start(bf16[288,1152]{1,0:T(8,128)(2,1)} %get-tuple-element.127), channel_id=1, source_target_pairs={{0,16},{8,24},{16,0},{24,8},{32,48},{40,56},{48,32},{56,40},{64,80... | collective-permute-start | bytes 1990664 | tf_op jit(solution)/shard_map/ppermute | solution.py:491
  128.8 6.6 %down_later.1 = (f32[288,1152]{1,0:T(8,128)S(1)}, f32[288,1152]{1,0:T(8,128)S(1)}, bf16[288,1152]{1,0:T(8,128)(2,1)S(1)}, bf16[288,1152]{1,0:T(8,128)(2,1)S(1)}, f32[288,1152]{1,0:T(8,128)S(1)}) custom-call(s32[5]{0:T(128)S(1)} %stack.54.s_ref, f32[8,128]{1,0:T(8,128)S(1)} %add.152.p_ref, f32[8,128]{1,0:T(8,128)S(1)} %collective-permute-done.15.q_ref, ...), custom_call_target="tpu_custom_call" | custom-call | flops 1000 | bytes 1000 | tf_op jit(solution)/shard_map/down_later/pallas_call | solution.py:313
  135.4 2.4 %down_join.1 = (bf16[288,1152]{1,0:T(8,128)(2,1)S(1)}, bf16[144,1152]{1,0:T(8,128)(2,1)S(1)}, bf16[144,1152]{1,0:T(8,128)(2,1)S(1)}) custom-call(f32[288,1152]{1,0:T(8,128)S(1)} %get-tuple-element.132.refs_0_, f32[288,1152]{1,0:T(8,128)S(1)} %get-tuple-element.133.refs_1_, bf16[288,1152]{1,0:T(8,128)(2,1)} %collective-permute-done.16.refs_2_, ...), custom_call_target="tpu_custom_call" | custom-call | flops 1000 | bytes 1000 | tf_op jit(solution)/shard_map/down_join/pallas_call | solution.py:400
  139.9 2.6 %up_join.1 = (bf16[288,1152]{1,0:T(8,128)(2,1)S(1)}, bf16[144,1152]{1,0:T(8,128)(2,1)S(1)}, bf16[144,1152]{1,0:T(8,128)(2,1)S(1)}) custom-call(f32[288,1152]{1,0:T(8,128)} %get-tuple-element.138.refs_0_, f32[288,1152]{1,0:T(8,128)} %get-tuple-element.139.refs_1_, bf16[288,1152]{1,0:T(8,128)(2,1)} %collective-permute-done.22.refs_2_, ...), custom_call_target="tpu_custom_call" | custom-call | flops 1000 | bytes 1000 | tf_op jit(solution)/shard_map/up_join/pallas_call | solution.py:400
  144.4 2.4 %collective-permute-start.27 = (bf16[288,1152]{1,0:T(8,128)(2,1)S(1)}, bf16[288,1152]{1,0:T(8,128)(2,1)S(1)}, u32[]{:S(2)}, u32[]{:S(2)}) collective-permute-start(bf16[288,1152]{1,0:T(8,128)(2,1)S(1)} %get-tuple-element.155), channel_id=1, source_target_pairs={{0,16},{8,24},{16,0},{24,8},{32,48},{40,56},{48,32},{56,40},{64,80... | collective-permute-start | bytes 1990664 | tf_op jit(solution)/shard_map/ppermute | solution.py:491
  146.8 3.5 %collective-permute-done.21.refs_1_ = bf16[288,1152]{1,0:T(8,128)(2,1)S(1)} collective-permute-done((bf16[288,1152]{1,0:T(8,128)(2,1)S(1)}, bf16[288,1152]{1,0:T(8,128)(2,1)S(1)}, u32[]{:S(2)}, u32[]{:S(2)}) %collective-permute-start.21) | collective-permute-done | bytes 663584 | tf_op jit(solution)/shard_map/ppermute | solution.py:491
  158.2 6.4 %collective-permute-done.27.refs_5_ = bf16[288,1152]{1,0:T(8,128)(2,1)S(1)} collective-permute-done((bf16[288,1152]{1,0:T(8,128)(2,1)S(1)}, bf16[288,1152]{1,0:T(8,128)(2,1)S(1)}, u32[]{:S(2)}, u32[]{:S(2)}) %collective-permute-start.27) | collective-permute-done | bytes 663584 | tf_op jit(solution)/shard_map/ppermute | solution.py:491
  165.6 9.0 %collective-permute-done.31.refs_7_ = bf16[288,1152]{1,0:T(8,128)(2,1)S(1)} collective-permute-done((bf16[288,1152]{1,0:T(8,128)(2,1)S(1)}, bf16[288,1152]{1,0:T(8,128)(2,1)S(1)}, u32[]{:S(2)}, u32[]{:S(2)}) %collective-permute-start.31) | collective-permute-done | bytes 663584 | tf_op jit(solution)/shard_map/ppermute | solution.py:491
  177.8 10.8 %collective-permute-start.32 = (bf16[288,1152]{1,0:T(8,128)(2,1)S(1)}, bf16[288,1152]{1,0:T(8,128)(2,1)S(1)}, u32[]{:S(2)}, u32[]{:S(2)}) collective-permute-start(bf16[288,1152]{1,0:T(8,128)(2,1)S(1)} %get-tuple-element.169), channel_id=1, source_target_pairs={{0,8},{8,0},{16,24},{24,16},{32,40},{40,32},{48,56},{56,48},{64,72... | collective-permute-start | bytes 1990664 | tf_op jit(solution)/shard_map/ppermute | solution.py:491
  (113 shorter events, 51.4 us)
Async XLA Ops:
  5.6 15.2 %collective-permute-start.1 = (bf16[768,2304]{1,0:T(8,128)(2,1)}, bf16[768,2304]{1,0:T(8,128)(2,1)}, u32[]{:S(2)}, u32[]{:S(2)}) collective-permute-start(bf16[768,2304]{1,0:T(8,128)(2,1)} %xa_hbm.1), channel_id=1, source_target_pairs={{0,8},{8,0},{16,24},{24,16},{32,40},{40,32},{48,56},{56,48},{64,72... | collective-permute-start | bytes 10616840 | tf_op jit(solution)/shard_map/ppermute | solution.py:491
  6.0 14.8 %collective-permute-start.2 = (bf16[768,2304]{1,0:T(8,128)(2,1)}, bf16[768,2304]{1,0:T(8,128)(2,1)}, u32[]{:S(2)}, u32[]{:S(2)}) collective-permute-start(bf16[768,2304]{1,0:T(8,128)(2,1)} %dy_hbm), channel_id=1, source_target_pairs={{0,8},{8,0},{16,24},{24,16},{32,40},{40,32},{48,56},{56,48},{64,72... | collective-permute-start | bytes 10616840 | tf_op jit(solution)/shard_map/ppermute | solution.py:491
  6.1 21.3 %collective-permute-start.5 = (bf16[288,1152]{1,0:T(8,128)(2,1)}, bf16[288,1152]{1,0:T(8,128)(2,1)}, u32[]{:S(2)}, u32[]{:S(2)}) collective-permute-start(bf16[288,1152]{1,0:T(8,128)(2,1)} %maximum_select_fusion.rest_0_), channel_id=1, source_target_pairs={{0,16},{8,24},{16,0},{24,8},{32,48},{40,56},{48,32},{56,40},{64,80... | collective-permute-start | bytes 1990664 | tf_op jit(solution)/shard_map/ppermute | solution.py:491
  8.9 18.4 %collective-permute-start.4 = (bf16[288,1152]{1,0:T(8,128)(2,1)}, bf16[288,1152]{1,0:T(8,128)(2,1)}, u32[]{:S(2)}, u32[]{:S(2)}) collective-permute-start(bf16[288,1152]{1,0:T(8,128)(2,1)} %maximum_select_fusion.rest_0_), channel_id=1, source_target_pairs={{0,96},{8,104},{16,112},{24,120},{32,0},{40,8},{48,16},{56,24},{64... | collective-permute-start | bytes 1990664 | tf_op jit(solution)/shard_map/ppermute | solution.py:491
  12.7 17.0 %collective-permute-start.3 = (bf16[288,1152]{1,0:T(8,128)(2,1)}, bf16[288,1152]{1,0:T(8,128)(2,1)}, u32[]{:S(2)}, u32[]{:S(2)}) collective-permute-start(bf16[288,1152]{1,0:T(8,128)(2,1)} %maximum_select_fusion.rest_0_), channel_id=1, source_target_pairs={{0,32},{8,40},{16,48},{24,56},{32,64},{40,72},{48,80},{56,88},{64,... | collective-permute-start | bytes 1990664 | tf_op jit(solution)/shard_map/ppermute | solution.py:491
  29.7 22.6 %collective-permute-start.6 = (bf16[1536,1152]{1,0:T(8,128)(2,1)S(1)}, bf16[1536,1152]{1,0:T(8,128)(2,1)S(1)}, u32[]{:S(2)}, u32[]{:S(2)}) collective-permute-start(bf16[1536,1152]{1,0:T(8,128)(2,1)S(1)} %get-tuple-element.103), channel_id=1, source_target_pairs={{0,8},{8,0},{16,24},{24,16},{32,40},{40,32},{48,56},{56,48},{64,72... | collective-permute-start | bytes 10616840 | tf_op jit(solution)/shard_map/ppermute | solution.py:491
  32.6 19.2 %collective-permute-start.8 = (bf16[144,1152]{1,0:T(8,128)(2,1)S(1)}, bf16[144,1152]{1,0:T(8,128)(2,1)S(1)}, u32[]{:S(2)}, u32[]{:S(2)}) collective-permute-start(bf16[144,1152]{1,0:T(8,128)(2,1)S(1)} %get-tuple-element.104), channel_id=1, source_target_pairs={{0,96},{8,104},{16,112},{24,120},{32,0},{40,8},{48,16},{56,24},{64... | collective-permute-start | bytes 995336 | tf_op jit(solution)/shard_map/ppermute | solution.py:491
  32.7 19.1 %collective-permute-start.7 = (bf16[144,1152]{1,0:T(8,128)(2,1)S(1)}, bf16[144,1152]{1,0:T(8,128)(2,1)S(1)}, u32[]{:S(2)}, u32[]{:S(2)}) collective-permute-start(bf16[144,1152]{1,0:T(8,128)(2,1)S(1)} %get-tuple-element.99), channel_id=1, source_target_pairs={{0,32},{8,40},{16,48},{24,56},{32,64},{40,72},{48,80},{56,88},{64,... | collective-permute-start | bytes 995336 | tf_op jit(solution)/shard_map/ppermute | solution.py:491
  34.2 26.0 %collective-permute-start.10 = (bf16[288,1152]{1,0:T(8,128)(2,1)}, bf16[288,1152]{1,0:T(8,128)(2,1)S(1)}, u32[]{:S(2)}, u32[]{:S(2)}) collective-permute-start(bf16[288,1152]{1,0:T(8,128)(2,1)} %collective-permute-done.5.rest_3_), channel_id=1, source_target_pairs={{0,96},{8,104},{16,112},{24,120},{32,0},{40,8},{48,16},{56,24},{64... | collective-permute-start | bytes 1990664 | tf_op jit(solution)/shard_map/ppermute | solution.py:491
  35.5 27.8 %collective-permute-start.9 = (bf16[288,1152]{1,0:T(8,128)(2,1)}, bf16[288,1152]{1,0:T(8,128)(2,1)S(1)}, u32[]{:S(2)}, u32[]{:S(2)}) collective-permute-start(bf16[288,1152]{1,0:T(8,128)(2,1)} %collective-permute-done.5.rest_3_), channel_id=1, source_target_pairs={{0,32},{8,40},{16,48},{24,56},{32,64},{40,72},{48,80},{56,88},{64,... | collective-permute-start | bytes 1990664 | tf_op jit(solution)/shard_map/ppermute | solution.py:491
  51.9 16.9 %collective-permute-start.11 = (bf16[288,1152]{1,0:T(8,128)(2,1)S(1)}, bf16[288,1152]{1,0:T(8,128)(2,1)S(1)}, u32[]{:S(2)}, u32[]{:S(2)}) collective-permute-start(bf16[288,1152]{1,0:T(8,128)(2,1)S(1)} %constant_dynamic-update-slice_fusion.rest_4_.rest_0_), channel_id=1, source_target_pairs={{0,16},{8,24},{16,0},{24,8},{32,48},{40,56},{48,32},{56,40},{64,80... | collective-permute-start | bytes 1990664 | tf_op jit(solution)/shard_map/ppermute | solution.py:491
  96.3 24.9 %collective-permute-start.16 = (bf16[288,1152]{1,0:T(8,128)(2,1)}, bf16[288,1152]{1,0:T(8,128)(2,1)}, u32[]{:S(2)}, u32[]{:S(2)}) collective-permute-start(bf16[288,1152]{1,0:T(8,128)(2,1)} %get-tuple-element.120), channel_id=1, source_target_pairs={{0,32},{8,40},{16,48},{24,56},{32,64},{40,72},{48,80},{56,88},{64,... | collective-permute-start | bytes 1990664 | tf_op jit(solution)/shard_map/ppermute | solution.py:491
  96.3 27.5 %collective-permute-start.17 = (bf16[288,1152]{1,0:T(8,128)(2,1)}, bf16[288,1152]{1,0:T(8,128)(2,1)}, u32[]{:S(2)}, u32[]{:S(2)}) collective-permute-start(bf16[288,1152]{1,0:T(8,128)(2,1)} %get-tuple-element.121), channel_id=1, source_target_pairs={{0,96},{8,104},{16,112},{24,120},{32,0},{40,8},{48,16},{56,24},{64... | collective-permute-start | bytes 1990664 | tf_op jit(solution)/shard_map/ppermute | solution.py:491
  99.0 24.8 %collective-permute-start.18 = (bf16[288,1152]{1,0:T(8,128)(2,1)}, bf16[288,1152]{1,0:T(8,128)(2,1)}, u32[]{:S(2)}, u32[]{:S(2)}) collective-permute-start(bf16[288,1152]{1,0:T(8,128)(2,1)} %get-tuple-element.122), channel_id=1, source_target_pairs={{0,16},{8,24},{16,0},{24,8},{32,48},{40,56},{48,32},{56,40},{64,80... | collective-permute-start | bytes 1990664 | tf_op jit(solution)/shard_map/ppermute | solution.py:491
  118.4 20.1 %collective-permute-start.22 = (bf16[288,1152]{1,0:T(8,128)(2,1)}, bf16[288,1152]{1,0:T(8,128)(2,1)}, u32[]{:S(2)}, u32[]{:S(2)}) collective-permute-start(bf16[288,1152]{1,0:T(8,128)(2,1)} %get-tuple-element.140), channel_id=1, source_target_pairs={{0,32},{8,40},{16,48},{24,56},{32,64},{40,72},{48,80},{56,88},{64,... | collective-permute-start | bytes 1990664 | tf_op jit(solution)/shard_map/ppermute | solution.py:491
  118.5 21.4 %collective-permute-start.23 = (bf16[288,1152]{1,0:T(8,128)(2,1)}, bf16[288,1152]{1,0:T(8,128)(2,1)}, u32[]{:S(2)}, u32[]{:S(2)}) collective-permute-start(bf16[288,1152]{1,0:T(8,128)(2,1)} %get-tuple-element.141), channel_id=1, source_target_pairs={{0,96},{8,104},{16,112},{24,120},{32,0},{40,8},{48,16},{56,24},{64... | collective-permute-start | bytes 1990664 | tf_op jit(solution)/shard_map/ppermute | solution.py:491
  121.2 18.7 %collective-permute-start.24 = (bf16[288,1152]{1,0:T(8,128)(2,1)}, bf16[288,1152]{1,0:T(8,128)(2,1)}, u32[]{:S(2)}, u32[]{:S(2)}) collective-permute-start(bf16[288,1152]{1,0:T(8,128)(2,1)} %get-tuple-element.127), channel_id=1, source_target_pairs={{0,16},{8,24},{16,0},{24,8},{32,48},{40,56},{48,32},{56,40},{64,80... | collective-permute-start | bytes 1990664 | tf_op jit(solution)/shard_map/ppermute | solution.py:491
  137.8 12.6 %collective-permute-start.21 = (bf16[288,1152]{1,0:T(8,128)(2,1)S(1)}, bf16[288,1152]{1,0:T(8,128)(2,1)S(1)}, u32[]{:S(2)}, u32[]{:S(2)}) collective-permute-start(bf16[288,1152]{1,0:T(8,128)(2,1)S(1)} %get-tuple-element.137), channel_id=1, source_target_pairs={{0,16},{8,24},{16,0},{24,8},{32,48},{40,56},{48,32},{56,40},{64,80... | collective-permute-start | bytes 1990664 | tf_op jit(solution)/shard_map/ppermute | solution.py:491
  144.4 20.2 %collective-permute-start.27 = (bf16[288,1152]{1,0:T(8,128)(2,1)S(1)}, bf16[288,1152]{1,0:T(8,128)(2,1)S(1)}, u32[]{:S(2)}, u32[]{:S(2)}) collective-permute-start(bf16[288,1152]{1,0:T(8,128)(2,1)S(1)} %get-tuple-element.155), channel_id=1, source_target_pairs={{0,16},{8,24},{16,0},{24,8},{32,48},{40,56},{48,32},{56,40},{64,80... | collective-permute-start | bytes 1990664 | tf_op jit(solution)/shard_map/ppermute | solution.py:491
  152.0 13.6 %collective-permute-start.25 = (bf16[288,1152]{1,0:T(8,128)(2,1)S(1)}, bf16[288,1152]{1,0:T(8,128)(2,1)S(1)}, u32[]{:S(2)}, u32[]{:S(2)}) collective-permute-start(bf16[288,1152]{1,0:T(8,128)(2,1)S(1)} %get-tuple-element.153), channel_id=1, source_target_pairs={{0,32},{8,40},{16,48},{24,56},{32,64},{40,72},{48,80},{56,88},{64,... | collective-permute-start | bytes 1990664 | tf_op jit(solution)/shard_map/ppermute | solution.py:491
  154.2 10.3 %collective-permute-start.26 = (bf16[288,1152]{1,0:T(8,128)(2,1)S(1)}, bf16[288,1152]{1,0:T(8,128)(2,1)S(1)}, u32[]{:S(2)}, u32[]{:S(2)}) collective-permute-start(bf16[288,1152]{1,0:T(8,128)(2,1)S(1)} %get-tuple-element.154), channel_id=1, source_target_pairs={{0,96},{8,104},{16,112},{24,120},{32,0},{40,8},{48,16},{56,24},{64... | collective-permute-start | bytes 1990664 | tf_op jit(solution)/shard_map/ppermute | solution.py:491
  156.6 17.9 %collective-permute-start.31 = (bf16[288,1152]{1,0:T(8,128)(2,1)S(1)}, bf16[288,1152]{1,0:T(8,128)(2,1)S(1)}, u32[]{:S(2)}, u32[]{:S(2)}) collective-permute-start(bf16[288,1152]{1,0:T(8,128)(2,1)S(1)} %get-tuple-element.166), channel_id=1, source_target_pairs={{0,96},{8,104},{16,112},{24,120},{32,0},{40,8},{48,16},{56,24},{64... | collective-permute-start | bytes 1990664 | tf_op jit(solution)/shard_map/ppermute | solution.py:491
  157.4 19.2 %collective-permute-start.30 = (bf16[288,1152]{1,0:T(8,128)(2,1)S(1)}, bf16[288,1152]{1,0:T(8,128)(2,1)S(1)}, u32[]{:S(2)}, u32[]{:S(2)}) collective-permute-start(bf16[288,1152]{1,0:T(8,128)(2,1)S(1)} %get-tuple-element.161), channel_id=1, source_target_pairs={{0,32},{8,40},{16,48},{24,56},{32,64},{40,72},{48,80},{56,88},{64,... | collective-permute-start | bytes 1990664 | tf_op jit(solution)/shard_map/ppermute | solution.py:491
  177.8 12.6 %collective-permute-start.32 = (bf16[288,1152]{1,0:T(8,128)(2,1)S(1)}, bf16[288,1152]{1,0:T(8,128)(2,1)S(1)}, u32[]{:S(2)}, u32[]{:S(2)}) collective-permute-start(bf16[288,1152]{1,0:T(8,128)(2,1)S(1)} %get-tuple-element.169), channel_id=1, source_target_pairs={{0,8},{8,0},{16,24},{24,16},{32,40},{40,32},{48,56},{56,48},{64,72... | collective-permute-start | bytes 1990664 | tf_op jit(solution)/shard_map/ppermute | solution.py:491
  (30 other events, 343.6 us)
